TPU v7x, 32 devices: a whole 2x2x4 slice. The times are simulated.
32 devices in a mesh: track: 4 (over x, core), tile: 8 (over z, y).
Axes of the slice: x: 2, y: 2, z: 4, core: 2. Of those that a mesh axis runs over, the one named last changes fastest.
Arguments:
- panels: bfloat16 [32768, 1024], P(('track', 'tile')), may hold values from -6 to 6
- phases: float32 [2048], P(('track', 'tile')), may hold values from -3.140625 to 3.140625
- weight_tiles: bfloat16 [4, 1024, 512], replicated, may hold values from -0.015625 to 0.015625
- tile_class: int32 [128], P(('track', 'tile')), may hold values from 0 to 3
- send_slots: int32 [24576], P(('track', 'tile')), may hold values from -1 to 1023, as said below
- foot_slot: int32 [128, 512], P(('track', 'tile')), may hold values from 0 to 767, as said below
- foot_ping: int32 [128, 512], P(('track', 'tile')), may hold values from 0 to 2047, as said below
- tile_counts: int32 [128], P(('track', 'tile')), may hold values from 102 to 512, as said below
Outputs:
- image: float32 [128, 2, 1024], P(('track', 'tile'))
- ping_gradient: float32 [2048], P(('track', 'tile'))
Inputs may be any that keep to these rules, and one draw needn't show every extreme that they name: `send_slots`: entries name local panel rows of the sending device; an entry is -1 exactly where the track group of its offset (offset minus 1) lies outside the slice. `foot_slot`: the entries of one tile are distinct slots, each of which holds a panel. foot_ping[t, f] is the ping of the panel in slot foot_slot[t, f] of tile t's device. `tile_counts`: only the first tile_counts_t entries of tile t's footprint lists are used.
All inputs are finite; a program needn't handle non-finite values.
Results may differ from a plain program's by a relative error of at most 0.0065.
Values may be sent and summed in bfloat16 or wider, within the bound.
A program may use at most 128 MiB of HBM per device.

v0:
```python
import functools

import jax
import jax.numpy as jnp
from jax import lax
from jax.experimental import pallas as pl
from jax.experimental.pallas import tpu as pltpu
from jax.sharding import PartitionSpec as P

F32 = jnp.float32
BF16 = jnp.bfloat16
MESH = pl.DeviceIdType.MESH
CHUNK = 256
NT = (((1,), (1,)), ((), ()))


def sincos(x):
    q = jnp.floor(x * 0.6366197723675814 + 0.5)
    r = ((x - q * 1.5703125) - q * 4.837512969970703e-4) - q * 7.549789948768648e-8
    r2 = r * r
    s = r + r * r2 * (-1.6666654611e-1 + r2 * (8.3321608736e-3 + r2 * -1.9515295891e-4))
    c = 1.0 - 0.5 * r2 + r2 * r2 * (
        4.166664568298827e-2 + r2 * (-1.388731625493765e-3 + r2 * 2.443315711809948e-5)
    )
    n = q.astype(jnp.int32)
    odd = (n & 1) == 1
    sine = jnp.where(odd, c, s)
    cosine = jnp.where(odd, s, c)
    sine = jnp.where((n & 2) == 2, -sine, sine)
    cosine = jnp.where(((n + 1) & 2) == 2, -cosine, cosine)
    return sine, cosine


def pack(block):
    half = block.shape[2] // 2
    return jnp.concatenate([block[:, :, :half], block[:, :, half:]], axis=1).astype(BF16)


def unpack(block):
    wide = block.astype(F32)
    rows = wide.shape[1] // 2
    return jnp.concatenate([wide[:, :rows], wide[:, rows:]], axis=2)


def kernel(
    n_track, n_tile, tiles_here, ping_local, slots,
    panels, phase, weights, send_col, send_row, mask,
    image, gradient,
    rot, gath, e_r, e_i, z, om, q_coef, m_in, part_s, near_out, near_in, tile_out, tile_in, h_all,
    m_ss, m_rs, b_ss, b_rs, c_ss, c_rs, d_ss, d_rs, e_ss, e_rs,
):
    a = lax.axis_index("track")
    b = lax.axis_index("tile")
    rows_total, width = panels.shape
    bins = width // 2
    classes, pixels, _ = weights.shape
    chunks = pixels // CHUNK
    group_rows = 2 * tiles_here
    tile_rows = n_tile * group_rows
    rows_per_ping = rows_total // ping_local
    device = a * n_tile + b
    ping_total = n_track * n_tile * ping_local
    tile_total = n_track * n_tile * tiles_here
    ping_step = n_track / ping_total
    tile_step = n_track / tile_total
    centre = 0.5 * n_track
    inside = {0: a >= 1, 1: None, 2: a <= n_track - 2}

    def guarded(o, body):
        def run():
            body()
        if o == 1:
            run()
        else:
            pl.when(inside[o])(run)

    def peer(track, tile):
        return {"track": track, "tile": tile}

    barrier = pltpu.get_barrier_semaphore()
    for o in range(3):
        def greet(o=o):
            def one(d, c):
                pl.semaphore_signal(
                    barrier, inc=1, device_id=peer(a + o - 1, lax.rem(b + d, n_tile)), device_id_type=MESH
                )
                return c
            lax.fori_loop(1 if o == 1 else 0, n_tile, one, 0)
        guarded(o, greet)

    def rotate(i, c):
        rows = pl.ds(pl.multiple_of(i * 128, 128), 128)
        sine, cosine = sincos(phase[rows, :])
        real = panels[rows, :bins].astype(F32)
        imag = panels[rows, bins:].astype(F32)
        rot[rows, :bins] = (cosine * real - sine * imag).astype(BF16)
        rot[rows, bins:] = (sine * real + cosine * imag).astype(BF16)
        return c

    lax.fori_loop(0, rows_total // 128, rotate, 0)

    neighbours = (
        n_tile - 1
        + n_tile * (jnp.where(a >= 1, 1, 0) + jnp.where(a <= n_track - 2, 1, 0))
    )
    pl.semaphore_wait(barrier, neighbours)

    def mask_copy(k, s):
        return pltpu.make_async_remote_copy(
            src_ref=mask.at[k, s], dst_ref=m_in.at[2 - k, b],
            send_sem=m_ss.at[k, s], recv_sem=m_rs.at[2 - k, b],
            device_id=peer(a + k - 1, s), device_id_type=MESH,
        )

    def mask_arrival(o, s):
        return pltpu.make_async_remote_copy(
            src_ref=mask.at[2 - o, s], dst_ref=m_in.at[o, s],
            send_sem=m_ss.at[2 - o, s], recv_sem=m_rs.at[o, s],
            device_id=peer(a + o - 1, s), device_id_type=MESH,
        )

    def each_peer(o, act):
        def one(d, c):
            act(lax.rem(b + d, n_tile))
            return c
        lax.fori_loop(1 if o == 1 else 0, n_tile, one, 0)

    for k in (0, 2, 1):
        guarded(k, lambda k=k: each_peer(k, lambda s: mask_copy(k, s).start()))
    m_in[1, b] = mask[1, b]
    for o in (0, 2):
        @pl.when(jnp.logical_not(inside[o]))
        def _(o=o):
            m_in[o] = jnp.zeros((n_tile, group_rows, slots), F32)
            h_all[o] = jnp.zeros((n_tile, 16, pixels // 2), BF16)

    def ping_places(rows):
        ping = device * ping_local + rows // rows_per_ping
        return (ping.astype(F32) + 0.5) * ping_step - centre

    def project(o):
        local = send_col[o]
        chosen = (lax.broadcasted_iota(jnp.int32, (slots, rows_total), 1) == local)
        chosen = jnp.where(chosen, 1.0, 0.0).astype(BF16)
        for half in range(2):
            for start in range(0, bins, CHUNK):
                column = half * bins + start
                got = jnp.dot(chosen, rot[:, column:column + CHUNK], preferred_element_type=F32)
                gath[half * slots:(half + 1) * slots, start:start + CHUNK] = got.astype(BF16)
        place = ping_places(local)
        lane = lax.broadcasted_iota(jnp.int32, (slots, CHUNK), 1).astype(F32)
        across = (lane + 0.5) * (1.0 / pixels) - 0.5
        now_i, now_r = sincos(96.0 * across * place + 8.0 * (place * place))
        step_i, step_r = sincos((96.0 * CHUNK / pixels) * place)
        for c in range(chunks):
            e_r[c] = now_r
            e_i[c] = now_i
            if c < chunks - 1:
                now_r, now_i = now_r * step_r - now_i * step_i, now_r * step_i + now_i * step_r

        def one(kc, carry):
            k = kc // chunks
            c = kc - k * chunks
            y = lax.dot_general(
                gath[...], weights[k, pl.ds(pl.multiple_of(c * CHUNK, CHUNK), CHUNK), :], NT,
                preferred_element_type=F32,
            )
            turn_r, turn_i = e_r[c], e_i[c]
            z[o, k, c, :slots] = (turn_r * y[:slots] - turn_i * y[slots:]).astype(BF16)
            z[o, k, c, slots:] = (turn_i * y[:slots] + turn_r * y[slots:]).astype(BF16)
            return carry

        lax.fori_loop(0, classes * chunks, one, 0)

    def partial_sums(o):
        guarded(o, lambda: each_peer(o, lambda s: mask_arrival(o, s).wait_recv()))
        marks = m_in[o].reshape(tile_rows, slots)
        row = lax.broadcasted_iota(jnp.int32, (tile_rows, slots), 0)
        group = row // group_rows
        real_row = (row - group * group_rows) < tiles_here
        tile = ((a + o - 1) * n_tile + group) * tiles_here + lax.rem(row, tiles_here)
        place = (tile.astype(F32) + 0.5) * tile_step - centre
        w_i, w_r = sincos(-16.0 * place * ping_places(send_row[o]))
        q_coef[o, :, :slots] = jnp.where(real_row, -w_i, w_r)
        q_coef[o, :, slots:] = jnp.where(real_row, -w_r, -w_i)
        coef = jnp.concatenate(
            [jnp.where(real_row, w_r, w_i), jnp.where(real_row, -w_i, w_r)], axis=1
        )
        marks = jnp.concatenate([marks, marks], axis=1)
        for k in range(classes):
            value = jnp.where(marks == k + 1.0, coef, 0.0)
            high = value.astype(BF16)
            om[k, :tile_rows] = high
            om[k, tile_rows:] = (value - high.astype(F32)).astype(BF16)
        for c in range(chunks):
            total = jnp.dot(om[0], z[o, 0, c], preferred_element_type=F32)
            for k in range(1, classes):
                total += jnp.dot(om[k], z[o, k, c], preferred_element_type=F32)
            total = total[:tile_rows] + total[tile_rows:]
            part_s[:, :, c * CHUNK:(c + 1) * CHUNK] = total.reshape(n_tile, group_rows, CHUNK)

    def near_copy(j):
        return pltpu.make_async_remote_copy(
            src_ref=near_out.at[j], dst_ref=near_in.at[j],
            send_sem=b_ss.at[j], recv_sem=b_rs.at[j],
            device_id=peer(a + 2 * j - 1, b), device_id_type=MESH,
        )

    for o in (0, 2):
        project(o)
        partial_sums(o)
        near_out[o // 2] = pack(part_s[...])
        guarded(o, lambda o=o: near_copy(o // 2).start())
    project(1)
    partial_sums(1)

    for j in range(2):
        def add(j=j):
            near_copy(j).wait_recv()
            part_s[...] += unpack(near_in[j])
        guarded(2 - 2 * j, add)
    tile_out[...] = pack(part_s[...])
    tile_in[b] = jnp.zeros((16, pixels // 2), BF16)

    def tile_copy(s, slot):
        return pltpu.make_async_remote_copy(
            src_ref=tile_out.at[s], dst_ref=tile_in.at[slot],
            send_sem=c_ss.at[s], recv_sem=c_rs.at[slot],
            device_id=peer(a, s), device_id_type=MESH,
        )

    each_peer(1, lambda s: tile_copy(s, b).start())
    each_peer(1, lambda s: tile_copy(s, s).wait_recv())
    arrived = unpack(tile_in[...])
    own = part_s[b]
    for s in range(n_tile):
        own = own + arrived[s]
    s_r, s_i = own[:tiles_here], own[tiles_here:]
    power = s_r * s_r + s_i * s_i
    heavy = jnp.concatenate([power * s_r, power * s_i], axis=0)
    h_all[1, b] = pack(heavy[None])[0]

    def h_copy(s, slot):
        return pltpu.make_async_remote_copy(
            src_ref=h_all.at[1, b], dst_ref=h_all.at[1, slot],
            send_sem=d_ss.at[s], recv_sem=d_rs.at[slot],
            device_id=peer(a, s), device_id_type=MESH,
        )

    def h_forward(o, s):
        return pltpu.make_async_remote_copy(
            src_ref=h_all.at[1, s], dst_ref=h_all.at[2 - o, s],
            send_sem=e_ss.at[o // 2, s], recv_sem=e_rs.at[o // 2, s],
            device_id=peer(a + o - 1, b), device_id_type=MESH,
        )

    each_peer(1, lambda s: h_copy(s, b).start())
    for o in (0, 2):
        guarded(o, lambda o=o: h_forward(o, b).start())

    tile_ids = device * tiles_here + lax.broadcasted_iota(jnp.int32, (tiles_here, pixels), 0)
    at = (tile_ids.astype(F32) + 0.5) * tile_step - centre
    lane = lax.broadcasted_iota(jnp.int32, (tiles_here, pixels), 1).astype(F32)
    across = (lane + 0.5) * (1.0 / pixels) - 0.5
    t_i, t_r = sincos(8.0 * (at * at) - 96.0 * across * at)
    out_r = t_r * s_r - t_i * s_i
    out_i = t_i * s_r + t_r * s_i
    for t in range(tiles_here):
        image[t, 0:1, :] = out_r[t:t + 1]
        image[t, 1:2, :] = out_i[t:t + 1]

    def relay(s):
        h_copy(s, s).wait_recv()
        for o in (0, 2):
            guarded(o, lambda o=o: h_forward(o, s).start())

    each_peer(1, relay)

    def pull(o):
        heavy = unpack(h_all[o]).reshape(tile_rows, pixels).astype(BF16)
        marks = m_in[o].reshape(tile_rows, slots)
        marks = jnp.concatenate([marks, marks], axis=1)
        total = jnp.zeros((tile_rows, 2 * slots), F32)
        for k in range(classes):
            got = lax.dot_general(heavy[:, :CHUNK], z[o, k, 0], NT, preferred_element_type=F32)
            for c in range(1, chunks):
                got += lax.dot_general(
                    heavy[:, c * CHUNK:(c + 1) * CHUNK], z[o, k, c], NT, preferred_element_type=F32
                )
            total = jnp.where(marks == k + 1.0, got, total)
        corr = jnp.sum(total * q_coef[o], axis=0, keepdims=True)
        corr = corr[:, :slots] + corr[:, slots:]
        ping = lax.broadcasted_iota(jnp.int32, (ping_local, slots), 0)
        return jnp.where(send_row[o] // rows_per_ping == ping, corr, 0.0)

    spread = pull(1)
    for o in (0, 2):
        guarded(o, lambda o=o: lax.fori_loop(
            0, n_tile, lambda s, c: (h_forward(2 - o, s).wait_recv(), c)[1], 0))
        spread = spread + pull(o)
    gradient[...] = jnp.sum(spread, axis=1, keepdims=True)

    for k in range(3):
        guarded(k, lambda k=k: each_peer(k, lambda s: mask_copy(k, s).wait_send()))
    for o in (0, 2):
        def finish(o=o):
            near_copy(o // 2).wait_send()
            lax.fori_loop(0, n_tile, lambda s, c: (h_forward(o, s).wait_send(), c)[1], 0)
        guarded(o, finish)
    each_peer(1, lambda s: tile_copy(s, b).wait_send())
    each_peer(1, lambda s: h_copy(s, b).wait_send())


def on_device(
    panels, phases, weight_tiles, tile_class, send_slots, foot_slot, foot_ping, tile_counts
):
    n_track = lax.axis_size("track")
    n_tile = lax.axis_size("tile")
    b = lax.axis_index("tile")
    ping_local = phases.shape[0]
    rows_total, width = panels.shape
    bins = width // 2
    tiles_here, foot = foot_slot.shape
    classes, pixels, _ = weight_tiles.shape
    slots = send_slots.shape[0] // 3
    cap = slots // n_tile
    group_rows = 2 * tiles_here
    tile_rows = n_tile * group_rows
    chunks = pixels // CHUNK

    used = jnp.arange(foot, dtype=jnp.int32)[None, :] < tile_counts[:, None]
    entries = jnp.where(used, foot_slot, -1)
    hit = entries[:, :, None] == jnp.arange(3 * slots, dtype=jnp.int32)[None, None, :]
    mark = jnp.where(hit.any(axis=1), (tile_class[:, None] + 1).astype(F32), 0.0)
    mark = mark.reshape(tiles_here, 3, n_tile, cap).transpose(1, 2, 0, 3)
    mark = jnp.tile(mark, (1, 1, 2, n_tile))
    mark = jnp.where(jnp.arange(slots) // cap == b, mark, 0.0)

    phase = jnp.repeat(phases, rows_total // ping_local)[:, None]
    vmem = pl.BlockSpec(memory_space=pltpu.VMEM)
    dma = pltpu.SemaphoreType.DMA
    image, gradient = pl.pallas_call(
        functools.partial(kernel, n_track, n_tile, tiles_here, ping_local, slots),
        out_shape=(
            jax.ShapeDtypeStruct((tiles_here, 2, pixels), F32),
            jax.ShapeDtypeStruct((ping_local, 1), F32),
        ),
        in_specs=[vmem] * 6,
        out_specs=(vmem, vmem),
        scratch_shapes=[
            pltpu.VMEM((rows_total, width), BF16),
            pltpu.VMEM((2 * slots, bins), BF16),
            pltpu.VMEM((chunks, slots, CHUNK), F32),
            pltpu.VMEM((chunks, slots, CHUNK), F32),
            pltpu.VMEM((3, classes, chunks, 2 * slots, CHUNK), BF16),
            pltpu.VMEM((classes, 2 * tile_rows, 2 * slots), BF16),
            pltpu.VMEM((3, tile_rows, 2 * slots), F32),
            pltpu.VMEM((3, n_tile, group_rows, slots), F32),
            pltpu.VMEM((n_tile, group_rows, pixels), F32),
            pltpu.VMEM((2, n_tile, 2 * group_rows, pixels // 2), BF16),
            pltpu.VMEM((2, n_tile, 2 * group_rows, pixels // 2), BF16),
            pltpu.VMEM((n_tile, 2 * group_rows, pixels // 2), BF16),
            pltpu.VMEM((n_tile, 2 * group_rows, pixels // 2), BF16),
            pltpu.VMEM((3, n_tile, 2 * group_rows, pixels // 2), BF16),
            dma((3, n_tile)), dma((3, n_tile)),
            dma((2,)), dma((2,)),
            dma((n_tile,)), dma((n_tile,)),
            dma((n_tile,)), dma((n_tile,)),
            dma((2, n_tile)), dma((2, n_tile)),
        ],
        compiler_params=pltpu.CompilerParams(
            collective_id=0, has_side_effects=True, vmem_limit_bytes=52 * 1024 * 1024
        ),
    )(
        panels, phase, weight_tiles,
        send_slots.reshape(3, slots, 1), send_slots.reshape(3, 1, slots), mark,
    )
    return image, gradient.reshape(ping_local)


def solution(mesh):
    in_specs = (
        P(("track", "tile"), None),
        P(("track", "tile")),
        P(),
        P(("track", "tile")),
        P(("track", "tile")),
        P(("track", "tile"), None),
        P(("track", "tile"), None),
        P(("track", "tile")),
    )
    out_specs = (P(("track", "tile"), None, None), P(("track", "tile")))
    return jax.shard_map(
        on_device, mesh=mesh, in_specs=in_specs, out_specs=out_specs, check_vma=False
    )
```

profile of v0, /device:TPU:1, one launch (start us, length us, event | category | flops | bytes accessed | tf_op | source)
XLA Modules:
  0.0 54.9 jit_solution(13187845412883566114)
XLA Ops:
  0.6 0.8 %fusion.1 = s32[4,512]{1,0:T(4,128)S(1)} fusion(s32[4,512]{1,0:T(4,128)} %param.13, s32[4]{0:T(128)} %param.14), kind=kLoop, calls=%fused_computation.5 | loop fusion | flops 4096 | bytes 16400 | tf_op jit(solution)/shard_map/jit(_where)/select_n | solution.py:332
  1.4 1.0 %fusion = pred[4,768]{1,0:T(4,128)(4,1)S(1)} fusion(s32[4,512]{1,0:T(4,128)S(1)} %fusion.1), kind=kLoop, calls=%fused_computation.1 | loop fusion | flops 3142656 | bytes 11264 | tf_op jit(solution)/shard_map/reduce_or | solution.py:334
  2.4 0.1 reduce_or.12
  2.5 0.7 %add_convert_fusion = f32[4]{0:T(128)S(1)} fusion(s32[4]{0:T(128)} %param.11), kind=kLoop, calls=%fused_computation.11 | loop fusion | flops 8 | bytes 32 | tf_op jit(solution)/shard_map/convert_element_type | solution.py:334
  3.2 0.1 select_bitcast_fusion
  3.3 0.1 tile.4
  3.4 0.2 tile.10
  3.7 0.7 %broadcast_in_dim.32 = f32[64,16]{1,0:T(8,128)S(1)} broadcast(f32[64]{0:T(128)} %param.9), dimensions={0} | broadcast | bytes 4352 | tf_op jit(solution)/shard_map/broadcast_in_dim | solution.py:339
  4.4 0.3 broadcast_in_dim_reshape.4.phase
  4.7 1.0 %reshape.32.send_col = s32[3,256,1]{2,1,0:T(8,128)S(1)} reshape(s32[768]{0:T(1024)} %param.12) | data formatting | bytes 6144 | tf_op jit(solution)/shard_map/reshape | solution.py:376
  5.7 0.7 %reshape.30.send_row = s32[3,1,256]{2,1,0:T(1,128)S(1)} reshape(s32[768]{0:T(1024)} %param.12) | data formatting | bytes 6144 | tf_op jit(solution)/shard_map/reshape | solution.py:376
  6.4 47.3 %shard_map.86 = (f32[4,2,1024]{2,1,0:T(2,128)S(1)}, f32[64,1]{1,0:T(8,128)S(1)}) custom-call(bf16[1024,1024]{1,0:T(8,128)(2,1)} %panels.1, f32[1024,1]{1,0:T(8,128)S(1)} %broadcast_in_dim_reshape.4.phase, bf16[4,1024,512]{2,1,0:T(8,128)(2,1)} %weights.1, s32[3,256,1]{2,1,0:T(8,128)S(1)} %reshape.32.send_col, s32[3,1,256]{2,1,0:T(1,128)S(1)} %reshape.30.send_row, ...), custom_call_target="tpu_custom_call" | custom-call | tf_op jit(solution)/shard_map/pallas_call | solution.py:342
  53.6 0.6 %reduce = f32[64]{0:T(128)} reduce(f32[64,1]{1,0:T(8,128)S(1)} %get-tuple-element.5, f32[]{:T(128)} %constant.31), dimensions={1}, to_apply=%get-tuple-element.5.reduce_sub_computation | reduce | bytes 516 | tf_op jit(solution)/shard_map/pallas_call | solution.py:342
  54.3 0.6 %copy.16 = f32[4,2,1024]{2,1,0:T(2,128)} copy(f32[4,2,1024]{2,1,0:T(2,128)S(1)} %get-tuple-element.8) | data formatting | bytes 65536
  (3 shorter events, 0.0 us)
where the time goes:
time: 55.6 us; the launch traced here: 54.9 us
  Pallas kernels  47.3 us (85%)
  local copies, waits for them, and re-layouts  3.73 us (7%)
  other arithmetic  3.17 us (6%)
  between operations  0.71 us (1%)
    pallas_call x1, Pallas kernels, on_device(): pl.pallas_call(functools.partial(kernel, n_track, n_tile, tiles_here, pin...  47.3 us

commit v1 on v0

v1 whole, which is shorter than its diff:
```python
import functools

import jax
import jax.numpy as jnp
from jax import lax
from jax.experimental import pallas as pl
from jax.experimental.pallas import tpu as pltpu
from jax.sharding import PartitionSpec as P

F32 = jnp.float32
BF16 = jnp.bfloat16
MESH = pl.DeviceIdType.MESH
CHUNK = 256
NT = (((1,), (1,)), ((), ()))


def sincos(x):
    q = jnp.floor(x * 0.6366197723675814 + 0.5)
    r = ((x - q * 1.5703125) - q * 4.837512969970703e-4) - q * 7.549789948768648e-8
    r2 = r * r
    s = r + r * r2 * (-1.6666654611e-1 + r2 * (8.3321608736e-3 + r2 * -1.9515295891e-4))
    c = 1.0 - 0.5 * r2 + r2 * r2 * (
        4.166664568298827e-2 + r2 * (-1.388731625493765e-3 + r2 * 2.443315711809948e-5)
    )
    n = q.astype(jnp.int32)
    odd = (n & 1) == 1
    sine = jnp.where(odd, c, s)
    cosine = jnp.where(odd, s, c)
    sine = jnp.where((n & 2) == 2, -sine, sine)
    cosine = jnp.where(((n + 1) & 2) == 2, -cosine, cosine)
    return sine, cosine


def pack(block):
    half = block.shape[2] // 2
    return jnp.concatenate([block[:, :, :half], block[:, :, half:]], axis=1).astype(BF16)


def unpack(block):
    wide = block.astype(F32)
    rows = wide.shape[1] // 2
    return jnp.concatenate([wide[:, :rows], wide[:, rows:]], axis=2)


def kernel(
    n_track, n_tile, tiles_here, ping_local, slots,
    classes_in, counts_in, panels_hbm, phases, weights_hbm, send_row, foot,
    image, gradient,
    panels, weights, column, gath, e_r, e_i, step_r, step_i, z, om, q_coef, q_sum, mark_out, m_in, marks,
    part, near_out, near_in, tile_out, tile_in, h_all,
    l_s, m_ss, m_rs, b_ss, b_rs, c_ss, c_rs, d_ss, d_rs, e_ss, e_rs,
):
    a = lax.axis_index("track")
    b = lax.axis_index("tile")
    rows_total, width = panels.shape
    bins = width // 2
    classes, pixels, _ = weights.shape
    chunks = pixels // CHUNK
    half = CHUNK // 2
    cap = slots // n_tile
    group_rows = 2 * tiles_here
    tile_rows = n_tile * group_rows
    rows_per_ping = rows_total // ping_local
    device = a * n_tile + b
    ping_total = n_track * n_tile * ping_local
    tile_total = n_track * n_tile * tiles_here
    ping_step = n_track / ping_total
    tile_step = n_track / tile_total
    centre = 0.5 * n_track
    inside = {0: a >= 1, 2: a <= n_track - 2}

    def guarded(o, body):
        def run():
            body()
        if o == 1:
            run()
        else:
            pl.when(inside[o])(run)

    def peer(track, tile):
        return {"track": track, "tile": tile}

    def each_peer(o, act):
        def one(d, c):
            act(lax.rem(b + d, n_tile))
            return c
        lax.fori_loop(1 if o == 1 else 0, n_tile, one, 0)

    panel_load = pltpu.make_async_copy(panels_hbm, panels, l_s.at[0])
    weight_load = pltpu.make_async_copy(weights_hbm, weights, l_s.at[1])
    panel_load.start()
    weight_load.start()

    barrier = pltpu.get_barrier_semaphore()
    for o in range(3):
        guarded(o, lambda o=o: each_peer(o, lambda s: pl.semaphore_signal(
            barrier, inc=1, device_id=peer(a + o - 1, s), device_id_type=MESH)))

    entry = lax.broadcasted_iota(jnp.int32, (1, foot.shape[1]), 1)
    used = []
    for t in range(tiles_here):
        used.append(jnp.where(entry < counts_in[t], foot[t:t + 1, :], -1))
    used = jnp.concatenate(used + used, axis=0).astype(F32)
    used = used.T
    slot_lane = lax.broadcasted_iota(jnp.int32, (foot.shape[1], 3 * slots), 1).astype(F32)
    for t in range(tiles_here):
        hit = jnp.where(used[:, t:t + 1] == slot_lane, 1.0, 0.0)
        hit = jnp.max(hit, axis=0, keepdims=True) * (classes_in[t] + 1).astype(F32)
        for k in range(3):
            mark_out[k, t:t + 1, :] = hit[:, k * slots:(k + 1) * slots]
            mark_out[k, tiles_here + t:tiles_here + t + 1, :] = hit[:, k * slots:(k + 1) * slots]

    neighbours = (
        n_tile - 1
        + n_tile * (jnp.where(a >= 1, 1, 0) + jnp.where(a <= n_track - 2, 1, 0))
    )
    pl.semaphore_wait(barrier, neighbours)

    def mark_copy(k, s, slot):
        return pltpu.make_async_remote_copy(
            src_ref=mark_out.at[k], dst_ref=m_in.at[2 - k, slot],
            send_sem=m_ss.at[k, s], recv_sem=m_rs.at[2 - k, slot],
            device_id=peer(a + k - 1, s), device_id_type=MESH,
        )

    for k in (0, 2, 1):
        guarded(k, lambda k=k: each_peer(k, lambda s: mark_copy(k, s, b).start()))
    m_in[1, b] = mark_out[1]
    for c in range(chunks):
        tile_in[c, b] = jnp.zeros((2 * group_rows, half), BF16)
    for o in (0, 2):
        @pl.when(jnp.logical_not(inside[o]))
        def _(o=o):
            m_in[o] = jnp.zeros((n_tile, group_rows, slots), F32)
            for c in range(chunks):
                h_all[c, o] = jnp.zeros((n_tile, 2 * group_rows, half), BF16)

    def ping_places(rows):
        ping = device * ping_local + rows // rows_per_ping
        return (ping.astype(F32) + 0.5) * ping_step - centre

    lines = jnp.broadcast_to(send_row[...].astype(F32), (8, 3 * slots))
    column[...] = lines.T[:, :1].astype(jnp.int32)
    panel_load.wait()

    def gather(o, carry):
        local = column[pl.ds(pl.multiple_of(o * slots, slots), slots), :]
        chosen = lax.broadcasted_iota(jnp.int32, (slots, rows_total), 1) == local
        chosen = jnp.where(chosen, 1.0, 0.0).astype(BF16)
        ping = lax.broadcasted_iota(jnp.int32, (slots, ping_local), 1)
        angle = jnp.where(ping == local // rows_per_ping, phases[...], 0.0)
        sine, cosine = sincos(jnp.sum(angle, axis=1, keepdims=True))
        for start in range(0, bins, CHUNK):
            real = jnp.dot(chosen, panels[:, start:start + CHUNK], preferred_element_type=F32)
            imag = jnp.dot(
                chosen, panels[:, bins + start:bins + start + CHUNK], preferred_element_type=F32
            )
            gath[o, :slots, start:start + CHUNK] = (cosine * real - sine * imag).astype(BF16)
            gath[o, slots:, start:start + CHUNK] = (sine * real + cosine * imag).astype(BF16)
        place = ping_places(local)
        lane = lax.broadcasted_iota(jnp.int32, (slots, CHUNK), 1).astype(F32)
        across = (lane + 0.5) * (1.0 / pixels) - 0.5
        first_i, first_r = sincos(96.0 * across * place + 8.0 * (place * place))
        e_r[o] = first_r
        e_i[o] = first_i
        turn_i, turn_r = sincos((96.0 * CHUNK / pixels) * place)
        step_r[o] = jnp.broadcast_to(turn_r, (slots, CHUNK))
        step_i[o] = jnp.broadcast_to(turn_i, (slots, CHUNK))
        return carry

    lax.fori_loop(0, 3, gather, 0)

    for o in range(3):
        guarded(o, lambda o=o: each_peer(o, lambda s: mark_copy(2 - o, s, s).wait_recv()))
    lane = lax.broadcasted_iota(jnp.int32, (group_rows, slots), 1)
    for o in range(3):
        for s in range(n_tile):
            shifted = pltpu.roll(m_in[o, s], lax.rem(s - b + n_tile, n_tile) * cap, 1)
            keep = (lane >= s * cap) & (lane < (s + 1) * cap)
            marks[o, s * group_rows:(s + 1) * group_rows, :slots] = jnp.where(keep, shifted, 0.0)
        mark = marks[o, :, :slots]
        marks[o, :, slots:] = mark
        row = lax.broadcasted_iota(jnp.int32, (tile_rows, slots), 0)
        group = row // group_rows
        real_row = (row - group * group_rows) < tiles_here
        tile = ((a + o - 1) * n_tile + group) * tiles_here + lax.rem(row, tiles_here)
        place = (tile.astype(F32) + 0.5) * tile_step - centre
        line = send_row[:, o * slots:(o + 1) * slots]
        w_i, w_r = sincos(-16.0 * place * ping_places(line))
        q_coef[o, :, :slots] = jnp.where(real_row, -w_i, w_r)
        q_coef[o, :, slots:] = jnp.where(real_row, -w_r, -w_i)
        coef = jnp.concatenate(
            [jnp.where(real_row, w_r, w_i), jnp.where(real_row, -w_i, w_r)], axis=1
        )
        mark = jnp.concatenate([mark, mark], axis=1)
        for k in range(classes):
            value = jnp.where(mark == k + 1.0, coef, 0.0)
            high = value.astype(BF16)
            om[o, k, :tile_rows] = high
            om[o, k, tile_rows:] = (value - high.astype(F32)).astype(BF16)
    q_sum[...] = jnp.zeros_like(q_sum)
    weight_load.wait()

    def near_copy(c, j):
        return pltpu.make_async_remote_copy(
            src_ref=near_out.at[c, j], dst_ref=near_in.at[c, j],
            send_sem=b_ss.at[c, j], recv_sem=b_rs.at[c, j],
            device_id=peer(a + 2 * j - 1, b), device_id_type=MESH,
        )

    def tile_copy(c, s, slot):
        return pltpu.make_async_remote_copy(
            src_ref=tile_out.at[c, s], dst_ref=tile_in.at[c, slot],
            send_sem=c_ss.at[c, s], recv_sem=c_rs.at[c, slot],
            device_id=peer(a, s), device_id_type=MESH,
        )

    def h_copy(c, s, slot):
        return pltpu.make_async_remote_copy(
            src_ref=h_all.at[c, 1, b], dst_ref=h_all.at[c, 1, slot],
            send_sem=d_ss.at[c, s], recv_sem=d_rs.at[c, slot],
            device_id=peer(a, s), device_id_type=MESH,
        )

    def h_forward(c, o, s):
        return pltpu.make_async_remote_copy(
            src_ref=h_all.at[c, 1, s], dst_ref=h_all.at[c, 2 - o, s],
            send_sem=e_ss.at[c, o // 2, s], recv_sem=e_rs.at[c, o // 2, s],
            device_id=peer(a + o - 1, b), device_id_type=MESH,
        )

    def project(c):
        totals = [None, None, None]
        for k in range(classes):
            weight = weights[k, pl.ds(pl.multiple_of(c * CHUNK, CHUNK), CHUNK), :]
            for o in (0, 2, 1):
                y = lax.dot_general(gath[o], weight, NT, preferred_element_type=F32)
                turn_r, turn_i = e_r[o], e_i[o]
                z[c, k, o, :slots] = (turn_r * y[:slots] - turn_i * y[slots:]).astype(BF16)
                z[c, k, o, slots:] = (turn_i * y[:slots] + turn_r * y[slots:]).astype(BF16)
                got = jnp.dot(om[o, k], z[c, k, o], preferred_element_type=F32)
                totals[o] = got if k == 0 else totals[o] + got
        for o in range(3):
            total = (totals[o][:tile_rows] + totals[o][tile_rows:]).reshape(n_tile, group_rows, CHUNK)
            if o == 1:
                part[c] = total
            else:
                near_out[c, o // 2] = pack(total)
        for o in (0, 2):
            guarded(o, lambda o=o: near_copy(c, o // 2).start())
        for o in range(3):
            now_r, now_i, by_r, by_i = e_r[o], e_i[o], step_r[o], step_i[o]
            e_r[o] = now_r * by_r - now_i * by_i
            e_i[o] = now_r * by_i + now_i * by_r

    def reduce_tracks(c):
        for j in range(2):
            def add(j=j):
                near_copy(c, j).wait_recv()
                part[c] += unpack(near_in[c, j])
            guarded(2 - 2 * j, add)
        tile_out[c] = pack(part[c])
        each_peer(1, lambda s: tile_copy(c, s, b).start())

    def reduce_tiles(c):
        each_peer(1, lambda s: tile_copy(c, s, s).wait_recv())
        arrived = unpack(tile_in[c])
        own = part[c, b]
        for s in range(n_tile):
            own = own + arrived[s]
        s_r, s_i = own[:tiles_here], own[tiles_here:]
        power = s_r * s_r + s_i * s_i
        heavy = jnp.concatenate([power * s_r, power * s_i], axis=0)
        h_all[c, 1, b] = pack(heavy[None])[0]
        each_peer(1, lambda s: h_copy(c, s, b).start())
        for o in (0, 2):
            guarded(o, lambda o=o: h_forward(c, o, b).start())
        tile_ids = device * tiles_here + lax.broadcasted_iota(jnp.int32, (tiles_here, CHUNK), 0)
        at = (tile_ids.astype(F32) + 0.5) * tile_step - centre
        pixel = c * CHUNK + lax.broadcasted_iota(jnp.int32, (tiles_here, CHUNK), 1)
        across = (pixel.astype(F32) + 0.5) * (1.0 / pixels) - 0.5
        t_i, t_r = sincos(8.0 * (at * at) - 96.0 * across * at)
        out_r = t_r * s_r - t_i * s_i
        out_i = t_i * s_r + t_r * s_i
        here = pl.ds(pl.multiple_of(c * CHUNK, CHUNK), CHUNK)
        for t in range(tiles_here):
            image[t, 0:1, here] = out_r[t:t + 1]
            image[t, 1:2, here] = out_i[t:t + 1]

    def relay(c):
        def one(s):
            h_copy(c, s, s).wait_recv()
            for o in (0, 2):
                guarded(o, lambda o=o: h_forward(c, o, s).start())
        each_peer(1, one)

    def pull(c):
        for o in (1, 0, 2):
            if o != 1:
                guarded(o, lambda o=o: lax.fori_loop(
                    0, n_tile, lambda s, x: (h_forward(c, 2 - o, s).wait_recv(), x)[1], 0))
            heavy = unpack(h_all[c, o]).reshape(tile_rows, CHUNK).astype(BF16)
            mark = marks[o]
            total = jnp.zeros((tile_rows, 2 * slots), F32)
            for k in range(classes):
                got = lax.dot_general(heavy, z[c, k, o], NT, preferred_element_type=F32)
                total = jnp.where(mark == k + 1.0, got, total)
            q_sum[o] += total

    def stage(i, carry):
        for lag, act in enumerate((project, reduce_tracks, reduce_tiles, relay, pull)):
            @pl.when((i >= lag) & (i < chunks + lag))
            def _(lag=lag, act=act):
                act(i - lag)
        return carry

    lax.fori_loop(0, chunks + 4, stage, 0)

    ping = lax.broadcasted_iota(jnp.int32, (ping_local, slots), 0)
    spread = jnp.zeros((ping_local, slots), F32)
    for o in range(3):
        corr = jnp.sum(q_sum[o] * q_coef[o], axis=0, keepdims=True)
        corr = corr[:, :slots] + corr[:, slots:]
        line = send_row[:, o * slots:(o + 1) * slots]
        spread = spread + jnp.where(line // rows_per_ping == ping, corr, 0.0)
    sums = jnp.sum(spread, axis=1, keepdims=True)
    gradient[...] = jnp.broadcast_to(sums, (ping_local, 128)).T[:1]

    for k in range(3):
        guarded(k, lambda k=k: each_peer(k, lambda s: mark_copy(k, s, b).wait_send()))

    def finish(c, carry):
        for o in (0, 2):
            def sent(o=o):
                near_copy(c, o // 2).wait_send()
                lax.fori_loop(0, n_tile, lambda s, x: (h_forward(c, o, s).wait_send(), x)[1], 0)
            guarded(o, sent)
        each_peer(1, lambda s: tile_copy(c, s, b).wait_send())
        each_peer(1, lambda s: h_copy(c, s, b).wait_send())
        return carry

    lax.fori_loop(0, chunks, finish, 0)


def on_device(
    panels, phases, weight_tiles, tile_class, send_slots, foot_slot, foot_ping, tile_counts
):
    n_track = lax.axis_size("track")
    n_tile = lax.axis_size("tile")
    ping_local = phases.shape[0]
    rows_total, width = panels.shape
    bins = width // 2
    tiles_here, foot = foot_slot.shape
    classes, pixels, _ = weight_tiles.shape
    slots = send_slots.shape[0] // 3
    group_rows = 2 * tiles_here
    tile_rows = n_tile * group_rows
    chunks = pixels // CHUNK
    packed = (n_tile, 2 * group_rows, CHUNK // 2)
    vmem = pl.BlockSpec(memory_space=pltpu.VMEM)
    smem = pl.BlockSpec(memory_space=pltpu.SMEM)
    hbm = pl.BlockSpec(memory_space=pl.ANY)
    dma = pltpu.SemaphoreType.DMA
    image, gradient = pl.pallas_call(
        functools.partial(kernel, n_track, n_tile, tiles_here, ping_local, slots),
        out_shape=(
            jax.ShapeDtypeStruct((tiles_here, 2, pixels), F32),
            jax.ShapeDtypeStruct((1, ping_local), F32),
        ),
        in_specs=[smem, smem, hbm, vmem, hbm, vmem, vmem],
        out_specs=(vmem, vmem),
        scratch_shapes=[
            pltpu.VMEM((rows_total, width), BF16),
            pltpu.VMEM((classes, pixels, bins), BF16),
            pltpu.VMEM((3 * slots, 1), jnp.int32),
            pltpu.VMEM((3, 2 * slots, bins), BF16),
            pltpu.VMEM((3, slots, CHUNK), F32),
            pltpu.VMEM((3, slots, CHUNK), F32),
            pltpu.VMEM((3, slots, CHUNK), F32),
            pltpu.VMEM((3, slots, CHUNK), F32),
            pltpu.VMEM((chunks, classes, 3, 2 * slots, CHUNK), BF16),
            pltpu.VMEM((3, classes, 2 * tile_rows, 2 * slots), BF16),
            pltpu.VMEM((3, tile_rows, 2 * slots), F32),
            pltpu.VMEM((3, tile_rows, 2 * slots), F32),
            pltpu.VMEM((3, group_rows, slots), F32),
            pltpu.VMEM((3, n_tile, group_rows, slots), F32),
            pltpu.VMEM((3, tile_rows, 2 * slots), F32),
            pltpu.VMEM((chunks, n_tile, group_rows, CHUNK), F32),
            pltpu.VMEM((chunks, 2) + packed, BF16),
            pltpu.VMEM((chunks, 2) + packed, BF16),
            pltpu.VMEM((chunks,) + packed, BF16),
            pltpu.VMEM((chunks,) + packed, BF16),
            pltpu.VMEM((chunks, 3) + packed, BF16),
            dma((2,)),
            dma((3, n_tile)), dma((3, n_tile)),
            dma((chunks, 2)), dma((chunks, 2)),
            dma((chunks, n_tile)), dma((chunks, n_tile)),
            dma((chunks, n_tile)), dma((chunks, n_tile)),
            dma((chunks, 2, n_tile)), dma((chunks, 2, n_tile)),
        ],
        compiler_params=pltpu.CompilerParams(
            collective_id=0, has_side_effects=True, vmem_limit_bytes=52 * 1024 * 1024
        ),
    )(
        tile_class, tile_counts, panels, phases.reshape(1, ping_local), weight_tiles,
        send_slots.reshape(1, 3 * slots), foot_slot,
    )
    return image, gradient.reshape(ping_local)


def solution(mesh):
    in_specs = (
        P(("track", "tile"), None),
        P(("track", "tile")),
        P(),
        P(("track", "tile")),
        P(("track", "tile")),
        P(("track", "tile"), None),
        P(("track", "tile"), None),
        P(("track", "tile")),
    )
    out_specs = (P(("track", "tile"), None, None), P(("track", "tile")))
    return jax.shard_map(
        on_device, mesh=mesh, in_specs=in_specs, out_specs=out_specs, check_vma=False
    )
```

time: 55.6 us -> 51.2 us (0.921)
  other arithmetic: 3.17 us -> 0 us
  Pallas kernels: 47.3 us -> 45.9 us
  local copies, waits for them, and re-layouts: 3.73 us -> 4.48 us
    unnamed x1 -> x10, local copies, waits for them, and re-layouts: 0.61 us -> 3.79 us
    pallas_call x1, Pallas kernels: 47.3 us -> 45.9 us  [on_device(): pl.pallas_call(functools.partial(kernel, n_track, n_tile, tiles_here, pin...]
    reduce_or x1 -> x0, other arithmetic: 1.01 us -> none  [on_device(): hit.any(axis=1)]
    reshape x2 -> x1, local copies, waits for them, and re-layouts: 1.65 us -> 0.69 us  [on_device(): send_slots.reshape(1, 3 * slots)]
    select_n x2 -> x0, other arithmetic: 0.79 us -> none  [the longest x1 0.77 us: on_device(): entries = jnp.where(used, foot_slot, -1)]
    broadcast_in_dim x1 -> x0, local copies, waits for them, and re-layouts: 0.73 us -> none  [on_device(): phase = jnp.repeat(phases, rows_total // ping_local)[:, None]]
    convert_element_type x1 -> x0, other arithmetic: 0.66 us -> none  [on_device(): (tile_class[:, None] + 1).astype(F32)]
    pallas_call x1 -> x0, other arithmetic: 0.63 us -> none  [on_device(): pl.pallas_call(functools.partial(kernel, n_track, n_tile, tiles_here, pin...]
where the time goes in v1:
time: 51.2 us; the launch traced here: 51 us
  Pallas kernels  45.9 us (90%)
  local copies, waits for them, and re-layouts  4.48 us (9%)
  between operations  0.64 us (1%)
    pallas_call x1, Pallas kernels, on_device(): pl.pallas_call(functools.partial(kernel, n_track, n_tile, tiles_here, pin...  45.9 us
    unnamed x10, local copies, waits for them, and re-layouts  3.79 us

profile of v1, /device:TPU:1, one launch (start us, length us, event | category | flops | bytes accessed | tf_op | source)
XLA Modules:
  0.0 51.0 jit_solution(446930071273215729)
XLA Ops:
  0.6 0.7 %reshape.14.send_row = s32[1,768]{1,0:T(1,128)S(1)} reshape(s32[768]{0:T(1024)} %param.12) | data formatting | bytes 6144 | tf_op jit(solution)/shard_map/reshape | solution.py:406
  1.3 0.0 copy-start
  1.3 0.7 %copy-done = s32[4,512]{1,0:T(4,128)S(1)} copy-done((s32[4,512]{1,0:T(4,128)S(1)}, s32[4,512]{1,0:T(4,128)}, u32[]{:S(2)}) %copy-start) | copy-done | bytes 8216
  2.0 0.0 copy-start.1
  2.0 0.7 %copy-done.1 = s32[4]{0:T(128)S(1)} copy-done((s32[4]{0:T(128)S(1)}, s32[4]{0:T(128)}, u32[]{:S(2)}) %copy-start.1) | copy-done | bytes 40
  2.7 0.0 copy-start.2
  2.7 0.7 %copy-done.2 = s32[4]{0:T(128)S(1)} copy-done((s32[4]{0:T(128)S(1)}, s32[4]{0:T(128)}, u32[]{:S(2)}) %copy-start.2) | copy-done | bytes 40
  3.3 0.0 copy-start.3
  3.3 0.7 %copy-done.3 = f32[64]{0:T(128)S(1)} copy-done((f32[64]{0:T(128)S(1)}, f32[64]{0:T(128)}, u32[]{:S(2)}) %copy-start.3) | copy-done | bytes 280
  4.0 45.9 %shard_map.86 = (f32[4,2,1024]{2,1,0:T(2,128)S(1)}, f32[1,64]{1,0:T(1,128)S(1)}) custom-call(s32[4]{0:T(128)S(1)} %copy-done.1, s32[4]{0:T(128)S(1)} %copy-done.2, bf16[1024,1024]{1,0:T(8,128)(2,1)} %panels_hbm.1, f32[1,64]{1,0:T(1,128)S(1)} %bitcast.2, bf16[4,1024,512]{2,1,0:T(8,128)(2,1)} %weights_hbm.1, s32[1,768]{1,0:T(1,128)S(1)} %reshape.14.send_row, ...), custom_call_target="tpu_custom_call" | custom-call | tf_op jit(solution)/shard_map/pallas_call | solution.py:364
  49.8 0.6 %copy.11 = f32[4,2,1024]{2,1,0:T(2,128)} copy(f32[4,2,1024]{2,1,0:T(2,128)S(1)} %get-tuple-element.8) | data formatting | bytes 65536
  50.5 0.5 %copy.12 = f32[64]{0:T(128)} copy(f32[64]{0:T(128)S(1)} %bitcast.3) | data formatting | bytes 512
Async XLA Ops:
  1.3 0.7 %copy-start = (s32[4,512]{1,0:T(4,128)S(1)}, s32[4,512]{1,0:T(4,128)}, u32[]{:S(2)}) copy-start(s32[4,512]{1,0:T(4,128)} %foot.1) | copy-start | bytes 24580
  2.0 0.7 %copy-start.1 = (s32[4]{0:T(128)S(1)}, s32[4]{0:T(128)}, u32[]{:S(2)}) copy-start(s32[4]{0:T(128)} %classes_in.1) | copy-start | bytes 52
  2.7 0.7 %copy-start.2 = (s32[4]{0:T(128)S(1)}, s32[4]{0:T(128)}, u32[]{:S(2)}) copy-start(s32[4]{0:T(128)} %counts_in.1) | copy-start | bytes 52
  3.3 0.7 %copy-start.3 = (f32[64]{0:T(128)S(1)}, f32[64]{0:T(128)}, u32[]{:S(2)}) copy-start(f32[64]{0:T(128)} %param.9) | copy-start | bytes 772

commit v2 on v1

v2 whole, which is shorter than its diff:
```python
import functools

import jax
import jax.numpy as jnp
from jax import lax
from jax.experimental import pallas as pl
from jax.experimental.pallas import tpu as pltpu
from jax.sharding import PartitionSpec as P

F32 = jnp.float32
BF16 = jnp.bfloat16
MESH = pl.DeviceIdType.MESH
CHUNK = 256
NT = (((1,), (1,)), ((), ()))


def sincos(x):
    q = jnp.floor(x * 0.6366197723675814 + 0.5)
    r = ((x - q * 1.5703125) - q * 4.837512969970703e-4) - q * 7.549789948768648e-8
    r2 = r * r
    s = r + r * r2 * (-1.6666654611e-1 + r2 * (8.3321608736e-3 + r2 * -1.9515295891e-4))
    c = 1.0 - 0.5 * r2 + r2 * r2 * (
        4.166664568298827e-2 + r2 * (-1.388731625493765e-3 + r2 * 2.443315711809948e-5)
    )
    n = q.astype(jnp.int32)
    odd = (n & 1) == 1
    sine = jnp.where(odd, c, s)
    cosine = jnp.where(odd, s, c)
    sine = jnp.where((n & 2) == 2, -sine, sine)
    cosine = jnp.where(((n + 1) & 2) == 2, -cosine, cosine)
    return sine, cosine


def pack(block):
    half = block.shape[2] // 2
    return jnp.concatenate([block[:, :, :half], block[:, :, half:]], axis=1).astype(BF16)


def unpack(block):
    wide = block.astype(F32)
    rows = wide.shape[1] // 2
    return jnp.concatenate([wide[:, :rows], wide[:, rows:]], axis=2)


def kernel(
    n_track, n_tile, tiles_here, ping_local, slots,
    classes_hbm, counts_hbm, panels_hbm, phases_hbm, weights_hbm, send_hbm, foot_hbm,
    image, gradient,
    classes_in, counts_in, panels, phases, weights, send, foot,
    column, gath, e_r, e_i, step_r, step_i, z, om, coef_t, mark_t, q_sum, mark_out, m_in,
    part, s_out, s_in, h_all,
    l_s, m_ss, m_rs, s_ss, s_rs, h_ss, h_rs,
):
    a = lax.axis_index("track")
    b = lax.axis_index("tile")
    rows_total, width = panels.shape
    bins = width // 2
    classes, pixels, _ = weights.shape
    chunks = pixels // CHUNK
    half = CHUNK // 2
    cap = slots // n_tile
    group_rows = 2 * tiles_here
    tile_rows = n_tile * group_rows
    rows_per_ping = rows_total // ping_local
    device = a * n_tile + b
    ping_total = n_track * n_tile * ping_local
    tile_total = n_track * n_tile * tiles_here
    ping_step = n_track / ping_total
    tile_step = n_track / tile_total
    centre = 0.5 * n_track
    inside = {0: a >= 1, 2: a <= n_track - 2}

    def guarded(o, body):
        def run():
            body()
        if o == 1:
            run()
        else:
            pl.when(inside[o])(run)

    def peer(track, tile):
        return {"track": track, "tile": tile}

    def each_peer(o, act):
        def one(d, c):
            act(lax.rem(b + d, n_tile))
            return c
        lax.fori_loop(1 if o == 1 else 0, n_tile, one, 0)

    loads = [
        pltpu.make_async_copy(source, target, l_s.at[n])
        for n, (source, target) in enumerate((
            (foot_hbm, foot), (counts_hbm, counts_in), (classes_hbm, classes_in), (send_hbm, send),
            (phases_hbm, phases), (panels_hbm, panels), (weights_hbm, weights),
        ))
    ]
    for load in loads:
        load.start()

    barrier = pltpu.get_barrier_semaphore()
    for o in range(3):
        guarded(o, lambda o=o: each_peer(o, lambda s: pl.semaphore_signal(
            barrier, inc=1, device_id=peer(a + o - 1, s), device_id_type=MESH)))

    for load in loads[:5]:
        load.wait()
    entry = lax.broadcasted_iota(jnp.int32, (1, foot.shape[1]), 1)
    used = []
    for t in range(tiles_here):
        used.append(jnp.where(entry < counts_in[t], foot[t:t + 1, :], -1))
    used = jnp.concatenate(used + used, axis=0).astype(F32)
    used = used.T
    slot_lane = lax.broadcasted_iota(jnp.int32, (foot.shape[1], 3 * slots), 1).astype(F32)
    for t in range(tiles_here):
        hit = jnp.where(used[:, t:t + 1] == slot_lane, 1.0, 0.0)
        hit = jnp.max(hit, axis=0, keepdims=True) * (classes_in[t] + 1).astype(F32)
        for k in range(3):
            mark_out[k, t:t + 1, :] = hit[:, k * slots:(k + 1) * slots]
            mark_out[k, tiles_here + t:tiles_here + t + 1, :] = hit[:, k * slots:(k + 1) * slots]

    neighbours = (
        n_tile - 1
        + n_tile * (jnp.where(a >= 1, 1, 0) + jnp.where(a <= n_track - 2, 1, 0))
    )
    pl.semaphore_wait(barrier, neighbours)

    def mark_copy(k, s, slot):
        return pltpu.make_async_remote_copy(
            src_ref=mark_out.at[k], dst_ref=m_in.at[2 - k, slot],
            send_sem=m_ss.at[k, s], recv_sem=m_rs.at[2 - k, slot],
            device_id=peer(a + k - 1, s), device_id_type=MESH,
        )

    for k in (0, 2, 1):
        guarded(k, lambda k=k: each_peer(k, lambda s: mark_copy(k, s, b).start()))
    m_in[1, b] = mark_out[1]
    blank = jnp.zeros((n_tile, 2 * group_rows, half), BF16)
    for c in range(chunks):
        s_in[c, 1, b] = blank[0]
    for o in (0, 2):
        @pl.when(jnp.logical_not(inside[o]))
        def _(o=o):
            m_in[o] = jnp.zeros((n_tile, group_rows, slots), F32)
            for c in range(chunks):
                h_all[c, o] = blank
                s_in[c, 2 - o] = blank

    def ping_places(rows):
        ping = device * ping_local + rows // rows_per_ping
        return (ping.astype(F32) + 0.5) * ping_step - centre

    line = jnp.concatenate([send[n:n + 1, :] for n in range(send.shape[0])], axis=1)
    owner = line // rows_per_ping
    phase = jnp.broadcast_to(phases[...], (8, ping_local)).T[:, :1]
    ping = lax.broadcasted_iota(jnp.int32, (ping_local, 3 * slots), 0)
    angle = jnp.sum(jnp.where(ping == owner, phase, 0.0), axis=0, keepdims=True)
    sine, cosine = sincos(angle)
    place = ping_places(line)
    half_i, half_r = sincos((96.0 * half / pixels) * place)
    full_i, full_r = sincos((96.0 * CHUNK / pixels) * place)
    lines = jnp.concatenate(
        [line.astype(F32), cosine, sine, place, half_r, half_i, full_r, full_i], axis=0
    )
    column[...] = lines.T
    loads[5].wait()

    def gather(o, carry):
        mine = column[pl.ds(pl.multiple_of(o * slots, slots), slots), :]
        local = mine[:, 0:1].astype(jnp.int32)
        chosen = lax.broadcasted_iota(jnp.int32, (slots, rows_total), 1) == local
        chosen = jnp.where(chosen, 1.0, 0.0).astype(BF16)
        cosine = jnp.broadcast_to(mine[:, 1:2], (slots, CHUNK))
        sine = jnp.broadcast_to(mine[:, 2:3], (slots, CHUNK))
        for start in range(0, bins, CHUNK):
            real = jnp.dot(chosen, panels[:, start:start + CHUNK], preferred_element_type=F32)
            imag = jnp.dot(
                chosen, panels[:, bins + start:bins + start + CHUNK], preferred_element_type=F32
            )
            gath[o, :slots, start:start + CHUNK] = (cosine * real - sine * imag).astype(BF16)
            gath[o, slots:, start:start + CHUNK] = (sine * real + cosine * imag).astype(BF16)
        place = mine[:, 3:4]
        lane = lax.broadcasted_iota(jnp.int32, (slots, half), 1).astype(F32)
        across = (lane + 0.5) * (1.0 / pixels) - 0.5
        first_i, first_r = sincos(96.0 * across * place + 8.0 * (place * place))
        half_r, half_i = mine[:, 4:5], mine[:, 5:6]
        e_r[o, :, :half] = first_r
        e_i[o, :, :half] = first_i
        e_r[o, :, half:] = first_r * half_r - first_i * half_i
        e_i[o, :, half:] = first_r * half_i + first_i * half_r
        step_r[o] = jnp.broadcast_to(mine[:, 6:7], (slots, CHUNK))
        step_i[o] = jnp.broadcast_to(mine[:, 7:8], (slots, CHUNK))
        return carry

    lax.fori_loop(0, 3, gather, 0)

    for o in range(3):
        guarded(o, lambda o=o: each_peer(o, lambda s: mark_copy(2 - o, s, s).wait_recv()))
    lane = lax.broadcasted_iota(jnp.int32, (group_rows, slots), 1)
    for o in range(3):
        mark = []
        for s in range(n_tile):
            shifted = pltpu.roll(m_in[o, s], lax.rem(s - b + n_tile, n_tile) * cap, 1)
            keep = (lane >= s * cap) & (lane < (s + 1) * cap)
            mark.append(jnp.where(keep, shifted, 0.0))
        mark = jnp.concatenate(mark, axis=0)
        row = lax.broadcasted_iota(jnp.int32, (tile_rows, slots), 0)
        group = row // group_rows
        real_row = (row - group * group_rows) < tiles_here
        tile = ((a + o - 1) * n_tile + group) * tiles_here + lax.rem(row, tiles_here)
        at = (tile.astype(F32) + 0.5) * tile_step - centre
        w_i, w_r = sincos(-16.0 * at * place[:, o * slots:(o + 1) * slots])
        mark_t[o] = mark.T
        coef_t[o, :slots] = jnp.where(real_row, -w_i, w_r).T
        coef_t[o, slots:] = jnp.where(real_row, -w_r, -w_i).T
        coef = jnp.concatenate(
            [jnp.where(real_row, w_r, w_i), jnp.where(real_row, -w_i, w_r)], axis=1
        )
        mark = jnp.concatenate([mark, mark], axis=1)
        for k in range(classes):
            value = jnp.where(mark == k + 1.0, coef, 0.0)
            high = value.astype(BF16)
            om[o, k, :tile_rows] = high
            om[o, k, tile_rows:] = (value - high.astype(F32)).astype(BF16)
    q_sum[...] = jnp.zeros_like(q_sum)
    loads[6].wait()

    def s_copy(c, o, s, slot):
        return pltpu.make_async_remote_copy(
            src_ref=s_out.at[c, o, s], dst_ref=s_in.at[c, o, slot],
            send_sem=s_ss.at[c, o, s], recv_sem=s_rs.at[c, o, slot],
            device_id=peer(a + o - 1, s), device_id_type=MESH,
        )

    def h_copy(c, o, s, slot):
        return pltpu.make_async_remote_copy(
            src_ref=h_all.at[c, 1, b], dst_ref=h_all.at[c, 2 - o, slot],
            send_sem=h_ss.at[c, o, s], recv_sem=h_rs.at[c, 2 - o, slot],
            device_id=peer(a + o - 1, s), device_id_type=MESH,
        )

    def project(c):
        totals = [None, None, None]
        for k in range(classes):
            weight = weights[k, pl.ds(pl.multiple_of(c * CHUNK, CHUNK), CHUNK), :]
            y = lax.dot_general(
                gath[...].reshape(6 * slots, bins), weight, NT, preferred_element_type=F32
            )
            for o in (0, 2, 1):
                real = y[2 * o * slots:(2 * o + 1) * slots]
                imag = y[(2 * o + 1) * slots:(2 * o + 2) * slots]
                turn_r, turn_i = e_r[o], e_i[o]
                turned = jnp.concatenate(
                    [turn_r * real - turn_i * imag, turn_i * real + turn_r * imag], axis=0
                ).astype(BF16)
                z[c, o, k] = turned
                got = jnp.dot(om[o, k], turned, preferred_element_type=F32)
                totals[o] = got if k == 0 else totals[o] + got
        for o in (0, 2, 1):
            total = (totals[o][:tile_rows] + totals[o][tile_rows:]).reshape(n_tile, group_rows, CHUNK)
            if o == 1:
                part[c] = total
            s_out[c, o] = pack(total)
            guarded(o, lambda o=o: each_peer(o, lambda s: s_copy(c, o, s, b).start()))
        for o in range(3):
            now_r, now_i, by_r, by_i = e_r[o], e_i[o], step_r[o], step_i[o]
            e_r[o] = now_r * by_r - now_i * by_i
            e_i[o] = now_r * by_i + now_i * by_r

    def reduce_tiles(c):
        for o in range(3):
            guarded(2 - o, lambda o=o: each_peer(o, lambda s: s_copy(c, o, s, s).wait_recv()))
        arrived = s_in[c].reshape(3 * n_tile, 2 * group_rows, half).astype(F32)
        own = part[c, b] + unpack(jnp.sum(arrived, axis=0, keepdims=True))[0]
        s_r, s_i = own[:tiles_here], own[tiles_here:]
        power = s_r * s_r + s_i * s_i
        heavy = jnp.concatenate([power * s_r, power * s_i], axis=0)
        h_all[c, 1, b] = pack(heavy[None])[0]
        for o in (0, 2, 1):
            guarded(o, lambda o=o: each_peer(o, lambda s: h_copy(c, o, s, b).start()))
        tile_ids = device * tiles_here + lax.broadcasted_iota(jnp.int32, (tiles_here, CHUNK), 0)
        at = (tile_ids.astype(F32) + 0.5) * tile_step - centre
        pixel = c * CHUNK + lax.broadcasted_iota(jnp.int32, (tiles_here, CHUNK), 1)
        across = (pixel.astype(F32) + 0.5) * (1.0 / pixels) - 0.5
        t_i, t_r = sincos(8.0 * (at * at) - 96.0 * across * at)
        out_r = t_r * s_r - t_i * s_i
        out_i = t_i * s_r + t_r * s_i
        here = pl.ds(pl.multiple_of(c * CHUNK, CHUNK), CHUNK)
        for t in range(tiles_here):
            image[t, 0:1, here] = out_r[t:t + 1]
            image[t, 1:2, here] = out_i[t:t + 1]

    def pull(c):
        for o in (1, 0, 2):
            guarded(o, lambda o=o: each_peer(o, lambda s: h_copy(c, 2 - o, s, s).wait_recv()))
            heavy = unpack(h_all[c, o]).reshape(tile_rows, CHUNK).astype(BF16)
            q_sum[o] += lax.dot_general(
                z[c, o].reshape(classes * 2 * slots, CHUNK), heavy, NT, preferred_element_type=F32
            )

    def stage(i, carry):
        for lag, act in enumerate((project, reduce_tiles, pull)):
            @pl.when((i >= lag) & (i < chunks + lag))
            def _(lag=lag, act=act):
                act(i - lag)
        return carry

    lax.fori_loop(0, chunks + 2, stage, 0)

    ping = lax.broadcasted_iota(jnp.int32, (slots, ping_local), 1)
    spread = jnp.zeros((slots, ping_local), F32)
    for o in range(3):
        mark = jnp.concatenate([mark_t[o], mark_t[o]], axis=0)
        total = jnp.zeros((2 * slots, tile_rows), F32)
        for k in range(classes):
            got = q_sum[o, k * 2 * slots:(k + 1) * 2 * slots]
            total = jnp.where(mark == k + 1.0, got, total)
        corr = jnp.sum(total * coef_t[o], axis=1, keepdims=True)
        corr = corr[:slots] + corr[slots:]
        local = column[o * slots:(o + 1) * slots, 0:1].astype(jnp.int32)
        spread = spread + jnp.where(local // rows_per_ping == ping, corr, 0.0)
    gradient[...] = jnp.sum(spread, axis=0, keepdims=True)

    for k in range(3):
        guarded(k, lambda k=k: each_peer(k, lambda s: mark_copy(k, s, b).wait_send()))

    def finish(c, carry):
        for o in range(3):
            guarded(o, lambda o=o: each_peer(o, lambda s: s_copy(c, o, s, b).wait_send()))
            guarded(o, lambda o=o: each_peer(o, lambda s: h_copy(c, o, s, b).wait_send()))
        return carry

    lax.fori_loop(0, chunks, finish, 0)


def on_device(
    panels, phases, weight_tiles, tile_class, send_slots, foot_slot, foot_ping, tile_counts
):
    n_track = lax.axis_size("track")
    n_tile = lax.axis_size("tile")
    ping_local = phases.shape[0]
    rows_total, width = panels.shape
    bins = width // 2
    tiles_here, foot = foot_slot.shape
    classes, pixels, _ = weight_tiles.shape
    slots = send_slots.shape[0] // 3
    group_rows = 2 * tiles_here
    tile_rows = n_tile * group_rows
    chunks = pixels // CHUNK
    packed = (n_tile, 2 * group_rows, CHUNK // 2)
    vmem = pl.BlockSpec(memory_space=pltpu.VMEM)
    hbm = pl.BlockSpec(memory_space=pl.ANY)
    dma = pltpu.SemaphoreType.DMA
    image, gradient = pl.pallas_call(
        functools.partial(kernel, n_track, n_tile, tiles_here, ping_local, slots),
        out_shape=(
            jax.ShapeDtypeStruct((tiles_here, 2, pixels), F32),
            jax.ShapeDtypeStruct((1, ping_local), F32),
        ),
        in_specs=[hbm] * 7,
        out_specs=(vmem, vmem),
        scratch_shapes=[
            pltpu.SMEM((tiles_here,), jnp.int32),
            pltpu.SMEM((tiles_here,), jnp.int32),
            pltpu.VMEM((rows_total, width), BF16),
            pltpu.VMEM((1, ping_local), F32),
            pltpu.VMEM((classes, pixels, bins), BF16),
            pltpu.VMEM((3 * slots // 128, 128), jnp.int32),
            pltpu.VMEM((tiles_here, foot), jnp.int32),
            pltpu.VMEM((3 * slots, 8), F32),
            pltpu.VMEM((3, 2 * slots, bins), BF16),
            pltpu.VMEM((3, slots, CHUNK), F32),
            pltpu.VMEM((3, slots, CHUNK), F32),
            pltpu.VMEM((3, slots, CHUNK), F32),
            pltpu.VMEM((3, slots, CHUNK), F32),
            pltpu.VMEM((chunks, 3, classes, 2 * slots, CHUNK), BF16),
            pltpu.VMEM((3, classes, 2 * tile_rows, 2 * slots), BF16),
            pltpu.VMEM((3, 2 * slots, tile_rows), F32),
            pltpu.VMEM((3, slots, tile_rows), F32),
            pltpu.VMEM((3, classes * 2 * slots, tile_rows), F32),
            pltpu.VMEM((3, group_rows, slots), F32),
            pltpu.VMEM((3, n_tile, group_rows, slots), F32),
            pltpu.VMEM((chunks, n_tile, group_rows, CHUNK), F32),
            pltpu.VMEM((chunks, 3) + packed, BF16),
            pltpu.VMEM((chunks, 3) + packed, BF16),
            pltpu.VMEM((chunks, 3) + packed, BF16),
            dma((7,)),
            dma((3, n_tile)), dma((3, n_tile)),
            dma((chunks, 3, n_tile)), dma((chunks, 3, n_tile)),
            dma((chunks, 3, n_tile)), dma((chunks, 3, n_tile)),
        ],
        compiler_params=pltpu.CompilerParams(
            collective_id=0, has_side_effects=True, vmem_limit_bytes=56 * 1024 * 1024
        ),
    )(
        tile_class, tile_counts, panels, phases.reshape(1, ping_local), weight_tiles,
        send_slots.reshape(3 * slots // 128, 128), foot_slot,
    )
    return image, gradient.reshape(ping_local)


def solution(mesh):
    in_specs = (
        P(("track", "tile"), None),
        P(("track", "tile")),
        P(),
        P(("track", "tile")),
        P(("track", "tile")),
        P(("track", "tile"), None),
        P(("track", "tile"), None),
        P(("track", "tile")),
    )
    out_specs = (P(("track", "tile"), None, None), P(("track", "tile")))
    return jax.shard_map(
        on_device, mesh=mesh, in_specs=in_specs, out_specs=out_specs, check_vma=False
    )
```

time: 51.2 us -> 53.6 us (1.047)
  Pallas kernels: 45.9 us -> 50.1 us
  local copies, waits for them, and re-layouts: 4.48 us -> 2.55 us
    pallas_call x1, Pallas kernels: 45.9 us -> 50.1 us  [on_device(): pl.pallas_call(functools.partial(kernel, n_track, n_tile, tiles_here, pin...]
    unnamed x10 -> x2, local copies, waits for them, and re-layouts: 3.79 us -> 2.55 us
    reshape x1 -> x0, local copies, waits for them, and re-layouts: 0.69 us -> none  [on_device(): send_slots.reshape(1, 3 * slots)]
where the time goes in v2:
time: 53.6 us; the launch traced here: 53.3 us
  Pallas kernels  50.1 us (93%)
  local copies, waits for them, and re-layouts  2.55 us (5%)
  between operations  0.64 us (1%)
    pallas_call x1, Pallas kernels, on_device(): pl.pallas_call(functools.partial(kernel, n_track, n_tile, tiles_here, pin...  50.1 us
    unnamed x2, local copies, waits for them, and re-layouts  2.55 us

profile of v2, /device:TPU:1, one launch (start us, length us, event | category | flops | bytes accessed | tf_op | source)
XLA Modules:
  0.0 53.3 jit_solution(14336030123306471328)
XLA Ops:
  0.6 50.1 %shard_map.86 = (f32[4,2,1024]{2,1,0:T(2,128)}, f32[1,64]{1,0:T(1,128)}) custom-call(s32[4]{0:T(128)} %classes_hbm.1, s32[4]{0:T(128)} %counts_hbm.1, bf16[1024,1024]{1,0:T(8,128)(2,1)} %panels_hbm.1, f32[1,64]{1,0:T(1,128)} %bitcast.4, bf16[4,1024,512]{2,1,0:T(8,128)(2,1)} %weights_hbm.1, s32[6,128]{1,0:T(8,128)} %bitcast.3, s32[4,512]{1,0:T(4,128)} %foot_hbm.1), custom_call_target="tpu_custom_call" | custom-call | tf_op jit(solution)/shard_map/pallas_call | solution.py:353
  50.8 1.4 %copy.11 = f32[4,2,1024]{2,1,0:T(2,128)} copy(f32[4,2,1024]{2,1,0:T(2,128)} %get-tuple-element.8) | data formatting | bytes 65536
  52.2 1.2 %copy.12 = f32[64]{0:T(128)} copy(f32[64]{0:T(128)} %bitcast.5) | data formatting | bytes 512

commit v3 on v1

--- a/solution.py
+++ b/solution.py
@@ -44,11 +44,12 @@
 
 def kernel(
     n_track, n_tile, tiles_here, ping_local, slots,
-    classes_in, counts_in, panels_hbm, phases, weights_hbm, send_row, foot,
+    classes_hbm, counts_hbm, panels_hbm, phases_hbm, weights_hbm, send_hbm, foot_hbm,
     image, gradient,
-    panels, weights, column, gath, e_r, e_i, step_r, step_i, z, om, q_coef, q_sum, mark_out, m_in, marks,
+    classes_in, counts_in, panels, phases, weights, send, foot,
+    column, gath, e_r, e_i, step_r, step_i, z, om, q_coef, q_sum, marks, mark_out, m_near, m_out, m_in,
     part, near_out, near_in, tile_out, tile_in, h_all,
-    l_s, m_ss, m_rs, b_ss, b_rs, c_ss, c_rs, d_ss, d_rs, e_ss, e_rs,
+    l_s, n_ss, n_rs, m_ss, m_rs, b_ss, b_rs, c_ss, c_rs, d_ss, d_rs, e_ss, e_rs,
 ):
     a = lax.axis_index("track")
     b = lax.axis_index("tile")
@@ -60,6 +61,7 @@
     cap = slots // n_tile
     group_rows = 2 * tiles_here
     tile_rows = n_tile * group_rows
+    mark_rows = m_out.shape[0]
     rows_per_ping = rows_total // ping_local
     device = a * n_tile + b
     ping_total = n_track * n_tile * ping_local
@@ -86,16 +88,23 @@
             return c
         lax.fori_loop(1 if o == 1 else 0, n_tile, one, 0)
 
-    panel_load = pltpu.make_async_copy(panels_hbm, panels, l_s.at[0])
-    weight_load = pltpu.make_async_copy(weights_hbm, weights, l_s.at[1])
-    panel_load.start()
-    weight_load.start()
+    loads = [
+        pltpu.make_async_copy(source, target, l_s.at[n])
+        for n, (source, target) in enumerate((
+            (foot_hbm, foot), (counts_hbm, counts_in), (classes_hbm, classes_in), (send_hbm, send),
+            (phases_hbm, phases), (panels_hbm, panels), (weights_hbm, weights),
+        ))
+    ]
+    for load in loads:
+        load.start()
 
     barrier = pltpu.get_barrier_semaphore()
     for o in range(3):
         guarded(o, lambda o=o: each_peer(o, lambda s: pl.semaphore_signal(
             barrier, inc=1, device_id=peer(a + o - 1, s), device_id_type=MESH)))
 
+    for load in loads[:5]:
+        load.wait()
     entry = lax.broadcasted_iota(jnp.int32, (1, foot.shape[1]), 1)
     used = []
     for t in range(tiles_here):
@@ -116,40 +125,59 @@
     )
     pl.semaphore_wait(barrier, neighbours)
 
-    def mark_copy(k, s, slot):
-        return pltpu.make_async_remote_copy(
-            src_ref=mark_out.at[k], dst_ref=m_in.at[2 - k, slot],
-            send_sem=m_ss.at[k, s], recv_sem=m_rs.at[2 - k, slot],
-            device_id=peer(a + k - 1, s), device_id_type=MESH,
-        )
-
-    for k in (0, 2, 1):
-        guarded(k, lambda k=k: each_peer(k, lambda s: mark_copy(k, s, b).start()))
-    m_in[1, b] = mark_out[1]
+    def mark_step(k):
+        return pltpu.make_async_remote_copy(
+            src_ref=mark_out.at[k], dst_ref=m_near.at[2 - k],
+            send_sem=n_ss.at[k], recv_sem=n_rs.at[2 - k],
+            device_id=peer(a + k - 1, b), device_id_type=MESH,
+        )
+
+    def mark_copy(s, slot):
+        return pltpu.make_async_remote_copy(
+            src_ref=m_out, dst_ref=m_in.at[slot],
+            send_sem=m_ss.at[s], recv_sem=m_rs.at[slot],
+            device_id=peer(a, s), device_id_type=MESH,
+        )
+
+    for k in (0, 2):
+        guarded(k, lambda k=k: mark_step(k).start())
+    m_near[1] = mark_out[1]
+    blank = jnp.zeros((n_tile, 2 * group_rows, half), BF16)
     for c in range(chunks):
-        tile_in[c, b] = jnp.zeros((2 * group_rows, half), BF16)
+        tile_in[c, b] = blank[0]
     for o in (0, 2):
         @pl.when(jnp.logical_not(inside[o]))
         def _(o=o):
-            m_in[o] = jnp.zeros((n_tile, group_rows, slots), F32)
+            m_near[o] = jnp.zeros((group_rows, slots), F32)
             for c in range(chunks):
-                h_all[c, o] = jnp.zeros((n_tile, 2 * group_rows, half), BF16)
+                h_all[c, o] = blank
 
     def ping_places(rows):
         ping = device * ping_local + rows // rows_per_ping
         return (ping.astype(F32) + 0.5) * ping_step - centre
 
-    lines = jnp.broadcast_to(send_row[...].astype(F32), (8, 3 * slots))
-    column[...] = lines.T[:, :1].astype(jnp.int32)
-    panel_load.wait()
+    line = jnp.concatenate([send[n:n + 1, :] for n in range(send.shape[0])], axis=1)
+    owner = line // rows_per_ping
+    phase = jnp.broadcast_to(phases[...], (8, ping_local)).T[:, :1]
+    ping = lax.broadcasted_iota(jnp.int32, (ping_local, 3 * slots), 0)
+    angle = jnp.sum(jnp.where(ping == owner, phase, 0.0), axis=0, keepdims=True)
+    sine, cosine = sincos(angle)
+    place = ping_places(line)
+    half_i, half_r = sincos((96.0 * half / pixels) * place)
+    full_i, full_r = sincos((96.0 * CHUNK / pixels) * place)
+    lines = jnp.concatenate(
+        [line.astype(F32), cosine, sine, place, half_r, half_i, full_r, full_i], axis=0
+    )
+    column[...] = lines.T
+    loads[5].wait()
 
     def gather(o, carry):
-        local = column[pl.ds(pl.multiple_of(o * slots, slots), slots), :]
+        mine = column[pl.ds(pl.multiple_of(o * slots, slots), slots), :]
+        local = mine[:, 0:1].astype(jnp.int32)
         chosen = lax.broadcasted_iota(jnp.int32, (slots, rows_total), 1) == local
         chosen = jnp.where(chosen, 1.0, 0.0).astype(BF16)
-        ping = lax.broadcasted_iota(jnp.int32, (slots, ping_local), 1)
-        angle = jnp.where(ping == local // rows_per_ping, phases[...], 0.0)
-        sine, cosine = sincos(jnp.sum(angle, axis=1, keepdims=True))
+        cosine = jnp.broadcast_to(mine[:, 1:2], (slots, CHUNK))
+        sine = jnp.broadcast_to(mine[:, 2:3], (slots, CHUNK))
         for start in range(0, bins, CHUNK):
             real = jnp.dot(chosen, panels[:, start:start + CHUNK], preferred_element_type=F32)
             imag = jnp.dot(
@@ -157,36 +185,49 @@
             )
             gath[o, :slots, start:start + CHUNK] = (cosine * real - sine * imag).astype(BF16)
             gath[o, slots:, start:start + CHUNK] = (sine * real + cosine * imag).astype(BF16)
-        place = ping_places(local)
-        lane = lax.broadcasted_iota(jnp.int32, (slots, CHUNK), 1).astype(F32)
+        place = mine[:, 3:4]
+        lane = lax.broadcasted_iota(jnp.int32, (slots, half), 1).astype(F32)
         across = (lane + 0.5) * (1.0 / pixels) - 0.5
         first_i, first_r = sincos(96.0 * across * place + 8.0 * (place * place))
-        e_r[o] = first_r
-        e_i[o] = first_i
-        turn_i, turn_r = sincos((96.0 * CHUNK / pixels) * place)
-        step_r[o] = jnp.broadcast_to(turn_r, (slots, CHUNK))
-        step_i[o] = jnp.broadcast_to(turn_i, (slots, CHUNK))
+        half_r, half_i = mine[:, 4:5], mine[:, 5:6]
+        e_r[o, :, :half] = first_r
+        e_i[o, :, :half] = first_i
+        e_r[o, :, half:] = first_r * half_r - first_i * half_i
+        e_i[o, :, half:] = first_r * half_i + first_i * half_r
+        step_r[o] = jnp.broadcast_to(mine[:, 6:7], (slots, CHUNK))
+        step_i[o] = jnp.broadcast_to(mine[:, 7:8], (slots, CHUNK))
         return carry
 
-    lax.fori_loop(0, 3, gather, 0)
-
+    gather(0, 0)
+    for o in (0, 2):
+        guarded(o, lambda o=o: mark_step(2 - o).wait_recv())
+    near = [m_near[o, :tiles_here] for o in range(3)]
+    near = jnp.concatenate(near + [jnp.zeros((mark_rows - 3 * tiles_here, slots), F32)], axis=0)
+    m_out[...] = near.astype(BF16)
+    m_in[b] = near.astype(BF16)
+    each_peer(1, lambda s: mark_copy(s, b).start())
+    lax.fori_loop(1, 3, gather, 0)
+
+    each_peer(1, lambda s: mark_copy(s, s).wait_recv())
+    lane = lax.broadcasted_iota(jnp.int32, (mark_rows, slots), 1)
+    got_marks = []
+    for s in range(n_tile):
+        shifted = pltpu.roll(m_in[s].astype(F32), lax.rem(s - b + n_tile, n_tile) * cap, 1)
+        got_marks.append(jnp.where((lane >= s * cap) & (lane < (s + 1) * cap), shifted, 0.0))
     for o in range(3):
-        guarded(o, lambda o=o: each_peer(o, lambda s: mark_copy(2 - o, s, s).wait_recv()))
-    lane = lax.broadcasted_iota(jnp.int32, (group_rows, slots), 1)
-    for o in range(3):
+        mark = []
         for s in range(n_tile):
-            shifted = pltpu.roll(m_in[o, s], lax.rem(s - b + n_tile, n_tile) * cap, 1)
-            keep = (lane >= s * cap) & (lane < (s + 1) * cap)
-            marks[o, s * group_rows:(s + 1) * group_rows, :slots] = jnp.where(keep, shifted, 0.0)
-        mark = marks[o, :, :slots]
-        marks[o, :, slots:] = mark
+            rows = got_marks[s][o * tiles_here:(o + 1) * tiles_here]
+            mark += [rows, rows]
+        mark = jnp.concatenate(mark, axis=0)
         row = lax.broadcasted_iota(jnp.int32, (tile_rows, slots), 0)
         group = row // group_rows
         real_row = (row - group * group_rows) < tiles_here
         tile = ((a + o - 1) * n_tile + group) * tiles_here + lax.rem(row, tiles_here)
-        place = (tile.astype(F32) + 0.5) * tile_step - centre
-        line = send_row[:, o * slots:(o + 1) * slots]
-        w_i, w_r = sincos(-16.0 * place * ping_places(line))
+        at = (tile.astype(F32) + 0.5) * tile_step - centre
+        w_i, w_r = sincos(-16.0 * at * place[:, o * slots:(o + 1) * slots])
+        marks[o, :, :slots] = mark
+        marks[o, :, slots:] = mark
         q_coef[o, :, :slots] = jnp.where(real_row, -w_i, w_r)
         q_coef[o, :, slots:] = jnp.where(real_row, -w_r, -w_i)
         coef = jnp.concatenate(
@@ -199,7 +240,7 @@
             om[o, k, :tile_rows] = high
             om[o, k, tile_rows:] = (value - high.astype(F32)).astype(BF16)
     q_sum[...] = jnp.zeros_like(q_sum)
-    weight_load.wait()
+    loads[6].wait()
 
     def near_copy(c, j):
         return pltpu.make_async_remote_copy(
@@ -222,10 +263,10 @@
             device_id=peer(a, s), device_id_type=MESH,
         )
 
-    def h_forward(c, o, s):
-        return pltpu.make_async_remote_copy(
-            src_ref=h_all.at[c, 1, s], dst_ref=h_all.at[c, 2 - o, s],
-            send_sem=e_ss.at[c, o // 2, s], recv_sem=e_rs.at[c, o // 2, s],
+    def h_forward(c, o):
+        return pltpu.make_async_remote_copy(
+            src_ref=h_all.at[c, 1], dst_ref=h_all.at[c, 2 - o],
+            send_sem=e_ss.at[c, o // 2], recv_sem=e_rs.at[c, o // 2],
             device_id=peer(a + o - 1, b), device_id_type=MESH,
         )
 
@@ -236,9 +277,12 @@
             for o in (0, 2, 1):
                 y = lax.dot_general(gath[o], weight, NT, preferred_element_type=F32)
                 turn_r, turn_i = e_r[o], e_i[o]
-                z[c, k, o, :slots] = (turn_r * y[:slots] - turn_i * y[slots:]).astype(BF16)
-                z[c, k, o, slots:] = (turn_i * y[:slots] + turn_r * y[slots:]).astype(BF16)
-                got = jnp.dot(om[o, k], z[c, k, o], preferred_element_type=F32)
+                turned = jnp.concatenate(
+                    [turn_r * y[:slots] - turn_i * y[slots:], turn_i * y[:slots] + turn_r * y[slots:]],
+                    axis=0,
+                ).astype(BF16)
+                z[c, o, k] = turned
+                got = jnp.dot(om[o, k], turned, preferred_element_type=F32)
                 totals[o] = got if k == 0 else totals[o] + got
         for o in range(3):
             total = (totals[o][:tile_rows] + totals[o][tile_rows:]).reshape(n_tile, group_rows, CHUNK)
@@ -273,8 +317,6 @@
         heavy = jnp.concatenate([power * s_r, power * s_i], axis=0)
         h_all[c, 1, b] = pack(heavy[None])[0]
         each_peer(1, lambda s: h_copy(c, s, b).start())
-        for o in (0, 2):
-            guarded(o, lambda o=o: h_forward(c, o, b).start())
         tile_ids = device * tiles_here + lax.broadcasted_iota(jnp.int32, (tiles_here, CHUNK), 0)
         at = (tile_ids.astype(F32) + 0.5) * tile_step - centre
         pixel = c * CHUNK + lax.broadcasted_iota(jnp.int32, (tiles_here, CHUNK), 1)
@@ -288,22 +330,19 @@
             image[t, 1:2, here] = out_i[t:t + 1]
 
     def relay(c):
-        def one(s):
-            h_copy(c, s, s).wait_recv()
-            for o in (0, 2):
-                guarded(o, lambda o=o: h_forward(c, o, s).start())
-        each_peer(1, one)
+        each_peer(1, lambda s: h_copy(c, s, s).wait_recv())
+        for o in (0, 2):
+            guarded(o, lambda o=o: h_forward(c, o).start())
 
     def pull(c):
         for o in (1, 0, 2):
             if o != 1:
-                guarded(o, lambda o=o: lax.fori_loop(
-                    0, n_tile, lambda s, x: (h_forward(c, 2 - o, s).wait_recv(), x)[1], 0))
+                guarded(o, lambda o=o: h_forward(c, 2 - o).wait_recv())
             heavy = unpack(h_all[c, o]).reshape(tile_rows, CHUNK).astype(BF16)
             mark = marks[o]
             total = jnp.zeros((tile_rows, 2 * slots), F32)
             for k in range(classes):
-                got = lax.dot_general(heavy, z[c, k, o], NT, preferred_element_type=F32)
+                got = lax.dot_general(heavy, z[c, o, k], NT, preferred_element_type=F32)
                 total = jnp.where(mark == k + 1.0, got, total)
             q_sum[o] += total
 
@@ -321,19 +360,20 @@
     for o in range(3):
         corr = jnp.sum(q_sum[o] * q_coef[o], axis=0, keepdims=True)
         corr = corr[:, :slots] + corr[:, slots:]
-        line = send_row[:, o * slots:(o + 1) * slots]
-        spread = spread + jnp.where(line // rows_per_ping == ping, corr, 0.0)
+        mine = line[:, o * slots:(o + 1) * slots]
+        spread = spread + jnp.where(mine // rows_per_ping == ping, corr, 0.0)
     sums = jnp.sum(spread, axis=1, keepdims=True)
     gradient[...] = jnp.broadcast_to(sums, (ping_local, 128)).T[:1]
 
-    for k in range(3):
-        guarded(k, lambda k=k: each_peer(k, lambda s: mark_copy(k, s, b).wait_send()))
+    for k in (0, 2):
+        guarded(k, lambda k=k: mark_step(k).wait_send())
+    each_peer(1, lambda s: mark_copy(s, b).wait_send())
 
     def finish(c, carry):
         for o in (0, 2):
             def sent(o=o):
                 near_copy(c, o // 2).wait_send()
-                lax.fori_loop(0, n_tile, lambda s, x: (h_forward(c, o, s).wait_send(), x)[1], 0)
+                h_forward(c, o).wait_send()
             guarded(o, sent)
         each_peer(1, lambda s: tile_copy(c, s, b).wait_send())
         each_peer(1, lambda s: h_copy(c, s, b).wait_send())
@@ -356,10 +396,10 @@
     group_rows = 2 * tiles_here
     tile_rows = n_tile * group_rows
     chunks = pixels // CHUNK
+    mark_rows = -(-3 * tiles_here // 16) * 16
     packed = (n_tile, 2 * group_rows, CHUNK // 2)
     vmem = pl.BlockSpec(memory_space=pltpu.VMEM)
-    smem = pl.BlockSpec(memory_space=pltpu.SMEM)
-    hbm = pl.BlockSpec(memory_space=pl.ANY)
+    hbm = pl.BlockSpec(memory_space=pltpu.HBM)
     dma = pltpu.SemaphoreType.DMA
     image, gradient = pl.pallas_call(
         functools.partial(kernel, n_track, n_tile, tiles_here, ping_local, slots),
@@ -367,43 +407,51 @@
             jax.ShapeDtypeStruct((tiles_here, 2, pixels), F32),
             jax.ShapeDtypeStruct((1, ping_local), F32),
         ),
-        in_specs=[smem, smem, hbm, vmem, hbm, vmem, vmem],
+        in_specs=[hbm] * 7,
         out_specs=(vmem, vmem),
         scratch_shapes=[
+            pltpu.SMEM((tiles_here,), jnp.int32),
+            pltpu.SMEM((tiles_here,), jnp.int32),
             pltpu.VMEM((rows_total, width), BF16),
+            pltpu.VMEM((1, ping_local), F32),
             pltpu.VMEM((classes, pixels, bins), BF16),
-            pltpu.VMEM((3 * slots, 1), jnp.int32),
+            pltpu.VMEM((3 * slots // 128, 128), jnp.int32),
+            pltpu.VMEM((tiles_here, foot), jnp.int32),
+            pltpu.VMEM((3 * slots, 8), F32),
             pltpu.VMEM((3, 2 * slots, bins), BF16),
             pltpu.VMEM((3, slots, CHUNK), F32),
             pltpu.VMEM((3, slots, CHUNK), F32),
             pltpu.VMEM((3, slots, CHUNK), F32),
             pltpu.VMEM((3, slots, CHUNK), F32),
-            pltpu.VMEM((chunks, classes, 3, 2 * slots, CHUNK), BF16),
+            pltpu.VMEM((chunks, 3, classes, 2 * slots, CHUNK), BF16),
             pltpu.VMEM((3, classes, 2 * tile_rows, 2 * slots), BF16),
             pltpu.VMEM((3, tile_rows, 2 * slots), F32),
             pltpu.VMEM((3, tile_rows, 2 * slots), F32),
+            pltpu.VMEM((3, tile_rows, 2 * slots), F32),
             pltpu.VMEM((3, group_rows, slots), F32),
-            pltpu.VMEM((3, n_tile, group_rows, slots), F32),
-            pltpu.VMEM((3, tile_rows, 2 * slots), F32),
+            pltpu.VMEM((3, group_rows, slots), F32),
+            pltpu.VMEM((mark_rows, slots), BF16),
+            pltpu.VMEM((n_tile, mark_rows, slots), BF16),
             pltpu.VMEM((chunks, n_tile, group_rows, CHUNK), F32),
             pltpu.VMEM((chunks, 2) + packed, BF16),
             pltpu.VMEM((chunks, 2) + packed, BF16),
             pltpu.VMEM((chunks,) + packed, BF16),
             pltpu.VMEM((chunks,) + packed, BF16),
             pltpu.VMEM((chunks, 3) + packed, BF16),
-            dma((2,)),
-            dma((3, n_tile)), dma((3, n_tile)),
+            dma((7,)),
+            dma((3,)), dma((3,)),
+            dma((n_tile,)), dma((n_tile,)),
             dma((chunks, 2)), dma((chunks, 2)),
             dma((chunks, n_tile)), dma((chunks, n_tile)),
             dma((chunks, n_tile)), dma((chunks, n_tile)),
-            dma((chunks, 2, n_tile)), dma((chunks, 2, n_tile)),
+            dma((chunks, 2)), dma((chunks, 2)),
         ],
         compiler_params=pltpu.CompilerParams(
-            collective_id=0, has_side_effects=True, vmem_limit_bytes=52 * 1024 * 1024
+            collective_id=0, has_side_effects=True, vmem_limit_bytes=48 * 1024 * 1024
         ),
     )(
         tile_class, tile_counts, panels, phases.reshape(1, ping_local), weight_tiles,
-        send_slots.reshape(1, 3 * slots), foot_slot,
+        send_slots.reshape(3 * slots // 128, 128), foot_slot,
     )
     return image, gradient.reshape(ping_local)
 

time: 51.2 us -> 51.9 us (1.014)
  local copies, waits for them, and re-layouts: 4.48 us -> 6.06 us
  Pallas kernels: 45.9 us -> 44.9 us
    unnamed x10 -> x14, local copies, waits for them, and re-layouts: 3.79 us -> 6.06 us
    pallas_call x1, Pallas kernels: 45.9 us -> 44.9 us  [on_device(): pl.pallas_call(functools.partial(kernel, n_track, n_tile, tiles_here, pin...]
    reshape x1 -> x0, local copies, waits for them, and re-layouts: 0.69 us -> none  [on_device(): send_slots.reshape(1, 3 * slots)]
where the time goes in v3:
time: 51.9 us; the launch traced here: 51.6 us
  Pallas kernels  44.9 us (87%)
  local copies, waits for them, and re-layouts  6.06 us (12%)
  between operations  0.65 us (1%)
    pallas_call x1, Pallas kernels, on_device(): pl.pallas_call(functools.partial(kernel, n_track, n_tile, tiles_here, pin...  44.9 us
    unnamed x14, local copies, waits for them, and re-layouts  6.06 us

profile of v3, /device:TPU:1, one launch (start us, length us, event | category | flops | bytes accessed | tf_op | source)
XLA Modules:
  0.0 51.6 jit_solution(6382145066501175988)
XLA Ops:
  0.6 0.0 copy-start
  0.6 1.6 %copy-done = bf16[1024,1024]{1,0:T(8,128)(2,1)S(1)} copy-done((bf16[1024,1024]{1,0:T(8,128)(2,1)S(1)}, bf16[1024,1024]{1,0:T(8,128)(2,1)}, u32[]{:S(2)}) %copy-start) | copy-done | bytes 2097176
  2.2 0.0 copy-start.1
  2.2 0.7 %copy-done.1 = s32[4,512]{1,0:T(4,128)S(1)} copy-done((s32[4,512]{1,0:T(4,128)S(1)}, s32[4,512]{1,0:T(4,128)}, u32[]{:S(2)}) %copy-start.1) | copy-done | bytes 8216
  2.9 0.0 copy-start.2
  2.9 0.7 %copy-done.2 = s32[768]{0:T(1024)S(1)} copy-done((s32[768]{0:T(1024)S(1)}, s32[768]{0:T(1024)}, u32[]{:S(2)}) %copy-start.2) | copy-done | bytes 3096
  3.6 0.0 copy-start.3
  3.6 0.7 %copy-done.3 = s32[4]{0:T(128)S(1)} copy-done((s32[4]{0:T(128)S(1)}, s32[4]{0:T(128)}, u32[]{:S(2)}) %copy-start.3) | copy-done | bytes 40
  4.3 0.0 copy-start.4
  4.3 0.7 %copy-done.4 = s32[4]{0:T(128)S(1)} copy-done((s32[4]{0:T(128)S(1)}, s32[4]{0:T(128)}, u32[]{:S(2)}) %copy-start.4) | copy-done | bytes 40
  4.9 0.0 copy-start.5
  4.9 0.7 %copy-done.5 = f32[64]{0:T(128)S(1)} copy-done((f32[64]{0:T(128)S(1)}, f32[64]{0:T(128)}, u32[]{:S(2)}) %copy-start.5) | copy-done | bytes 280
  5.6 44.9 %shard_map.86 = (f32[4,2,1024]{2,1,0:T(2,128)S(1)}, f32[1,64]{1,0:T(1,128)S(1)}) custom-call(s32[4]{0:T(128)S(1)} %copy-done.3, s32[4]{0:T(128)S(1)} %copy-done.4, bf16[1024,1024]{1,0:T(8,128)(2,1)S(1)} %copy-done, f32[1,64]{1,0:T(1,128)S(1)} %bitcast.4, bf16[4,1024,512]{2,1,0:T(8,128)(2,1)} %weights_hbm.1, s32[6,128]{1,0:T(8,128)S(1)} %bitcast.3, ...), custom_call_target="tpu_custom_call" | custom-call | tf_op jit(solution)/shard_map/pallas_call | solution.py:404
  50.5 0.6 %copy.11 = f32[4,2,1024]{2,1,0:T(2,128)} copy(f32[4,2,1024]{2,1,0:T(2,128)S(1)} %get-tuple-element.8) | data formatting | bytes 65536
  51.1 0.5 copy.12
Async XLA Ops:
  0.6 1.6 %copy-start = (bf16[1024,1024]{1,0:T(8,128)(2,1)S(1)}, bf16[1024,1024]{1,0:T(8,128)(2,1)}, u32[]{:S(2)}) copy-start(bf16[1024,1024]{1,0:T(8,128)(2,1)} %panels_hbm.1) | copy-start | bytes 6291460
  2.2 0.7 %copy-start.1 = (s32[4,512]{1,0:T(4,128)S(1)}, s32[4,512]{1,0:T(4,128)}, u32[]{:S(2)}) copy-start(s32[4,512]{1,0:T(4,128)} %foot_hbm.1) | copy-start | bytes 24580
  2.9 0.7 %copy-start.2 = (s32[768]{0:T(1024)S(1)}, s32[768]{0:T(1024)}, u32[]{:S(2)}) copy-start(s32[768]{0:T(1024)} %param.12) | copy-start | bytes 9220
  3.6 0.7 %copy-start.3 = (s32[4]{0:T(128)S(1)}, s32[4]{0:T(128)}, u32[]{:S(2)}) copy-start(s32[4]{0:T(128)} %classes_hbm.1) | copy-start | bytes 52
  4.3 0.7 %copy-start.4 = (s32[4]{0:T(128)S(1)}, s32[4]{0:T(128)}, u32[]{:S(2)}) copy-start(s32[4]{0:T(128)} %counts_hbm.1) | copy-start | bytes 52
  4.9 0.7 %copy-start.5 = (f32[64]{0:T(128)S(1)}, f32[64]{0:T(128)}, u32[]{:S(2)}) copy-start(f32[64]{0:T(128)} %param.9) | copy-start | bytes 772

commit v4 on v3

--- a/solution.py
+++ b/solution.py
@@ -83,10 +83,8 @@
         return {"track": track, "tile": tile}
 
     def each_peer(o, act):
-        def one(d, c):
+        for d in range(1 if o == 1 else 0, n_tile):
             act(lax.rem(b + d, n_tile))
-            return c
-        lax.fori_loop(1 if o == 1 else 0, n_tile, one, 0)
 
     loads = [
         pltpu.make_async_copy(source, target, l_s.at[n])
@@ -447,7 +445,7 @@
             dma((chunks, 2)), dma((chunks, 2)),
         ],
         compiler_params=pltpu.CompilerParams(
-            collective_id=0, has_side_effects=True, vmem_limit_bytes=48 * 1024 * 1024
+            collective_id=0, has_side_effects=True, vmem_limit_bytes=56 * 1024 * 1024
         ),
     )(
         tile_class, tile_counts, panels, phases.reshape(1, ping_local), weight_tiles,

time: 51.9 us -> 48.4 us (0.933)
  local copies, waits for them, and re-layouts: 6.06 us -> 2.55 us
    unnamed x14 -> x2, local copies, waits for them, and re-layouts: 6.06 us -> 2.55 us
where the time goes in v4:
time: 48.4 us; the launch traced here: 48.2 us
  Pallas kernels  45 us (93%)
  local copies, waits for them, and re-layouts  2.55 us (5%)
  between operations  0.64 us (1%)
    pallas_call x1, Pallas kernels, on_device(): pl.pallas_call(functools.partial(kernel, n_track, n_tile, tiles_here, pin...  45 us
    unnamed x2, local copies, waits for them, and re-layouts  2.55 us

profile of v4, /device:TPU:1, one launch (start us, length us, event | category | flops | bytes accessed | tf_op | source)
XLA Modules:
  0.0 48.2 jit_solution(6942585919153546789)
XLA Ops:
  0.6 45.0 %shard_map.86 = (f32[4,2,1024]{2,1,0:T(2,128)}, f32[1,64]{1,0:T(1,128)}) custom-call(s32[4]{0:T(128)} %classes_hbm.1, s32[4]{0:T(128)} %counts_hbm.1, bf16[1024,1024]{1,0:T(8,128)(2,1)} %panels_hbm.1, f32[1,64]{1,0:T(1,128)} %bitcast.4, bf16[4,1024,512]{2,1,0:T(8,128)(2,1)} %weights_hbm.1, s32[6,128]{1,0:T(8,128)} %bitcast.3, s32[4,512]{1,0:T(4,128)} %foot_hbm.1), custom_call_target="tpu_custom_call" | custom-call | tf_op jit(solution)/shard_map/pallas_call | solution.py:402
  45.6 1.4 %copy.11 = f32[4,2,1024]{2,1,0:T(2,128)} copy(f32[4,2,1024]{2,1,0:T(2,128)} %get-tuple-element.8) | data formatting | bytes 65536
  47.0 1.2 %copy.12 = f32[64]{0:T(128)} copy(f32[64]{0:T(128)} %bitcast.5) | data formatting | bytes 512

commit v5 on v4

--- a/solution.py
+++ b/solution.py
@@ -167,22 +167,9 @@
         [line.astype(F32), cosine, sine, place, half_r, half_i, full_r, full_i], axis=0
     )
     column[...] = lines.T
-    loads[5].wait()
-
-    def gather(o, carry):
+
+    def grids(o, carry):
         mine = column[pl.ds(pl.multiple_of(o * slots, slots), slots), :]
-        local = mine[:, 0:1].astype(jnp.int32)
-        chosen = lax.broadcasted_iota(jnp.int32, (slots, rows_total), 1) == local
-        chosen = jnp.where(chosen, 1.0, 0.0).astype(BF16)
-        cosine = jnp.broadcast_to(mine[:, 1:2], (slots, CHUNK))
-        sine = jnp.broadcast_to(mine[:, 2:3], (slots, CHUNK))
-        for start in range(0, bins, CHUNK):
-            real = jnp.dot(chosen, panels[:, start:start + CHUNK], preferred_element_type=F32)
-            imag = jnp.dot(
-                chosen, panels[:, bins + start:bins + start + CHUNK], preferred_element_type=F32
-            )
-            gath[o, :slots, start:start + CHUNK] = (cosine * real - sine * imag).astype(BF16)
-            gath[o, slots:, start:start + CHUNK] = (sine * real + cosine * imag).astype(BF16)
         place = mine[:, 3:4]
         lane = lax.broadcasted_iota(jnp.int32, (slots, half), 1).astype(F32)
         across = (lane + 0.5) * (1.0 / pixels) - 0.5
@@ -196,7 +183,7 @@
         step_i[o] = jnp.broadcast_to(mine[:, 7:8], (slots, CHUNK))
         return carry
 
-    gather(0, 0)
+    lax.fori_loop(0, 3, grids, 0)
     for o in (0, 2):
         guarded(o, lambda o=o: mark_step(2 - o).wait_recv())
     near = [m_near[o, :tiles_here] for o in range(3)]
@@ -204,7 +191,22 @@
     m_out[...] = near.astype(BF16)
     m_in[b] = near.astype(BF16)
     each_peer(1, lambda s: mark_copy(s, b).start())
-    lax.fori_loop(1, 3, gather, 0)
+
+    loads[5].wait()
+    local = column[:, 0:1].astype(jnp.int32)
+    chosen = lax.broadcasted_iota(jnp.int32, (3 * slots, rows_total), 1) == local
+    chosen = jnp.where(chosen, 1.0, 0.0).astype(BF16)
+    for start in range(0, bins, CHUNK):
+        real = jnp.dot(chosen, panels[:, start:start + CHUNK], preferred_element_type=F32)
+        imag = jnp.dot(
+            chosen, panels[:, bins + start:bins + start + CHUNK], preferred_element_type=F32
+        )
+        for o in range(3):
+            rows = slice(o * slots, (o + 1) * slots)
+            cosine = jnp.broadcast_to(column[rows, 1:2], (slots, CHUNK))
+            sine = jnp.broadcast_to(column[rows, 2:3], (slots, CHUNK))
+            gath[o, :slots, start:start + CHUNK] = (cosine * real[rows] - sine * imag[rows]).astype(BF16)
+            gath[o, slots:, start:start + CHUNK] = (sine * real[rows] + cosine * imag[rows]).astype(BF16)
 
     each_peer(1, lambda s: mark_copy(s, s).wait_recv())
     lane = lax.broadcasted_iota(jnp.int32, (mark_rows, slots), 1)
@@ -272,8 +274,11 @@
         totals = [None, None, None]
         for k in range(classes):
             weight = weights[k, pl.ds(pl.multiple_of(c * CHUNK, CHUNK), CHUNK), :]
+            every = lax.dot_general(
+                gath[...].reshape(6 * slots, bins), weight, NT, preferred_element_type=F32
+            )
             for o in (0, 2, 1):
-                y = lax.dot_general(gath[o], weight, NT, preferred_element_type=F32)
+                y = every[2 * o * slots:2 * (o + 1) * slots]
                 turn_r, turn_i = e_r[o], e_i[o]
                 turned = jnp.concatenate(
                     [turn_r * y[:slots] - turn_i * y[slots:], turn_i * y[:slots] + turn_r * y[slots:]],

time: 48.4 us -> 49.5 us (1.023)
  Pallas kernels: 45 us -> 46.1 us
    pallas_call x1, Pallas kernels: 45 us -> 46.1 us  [on_device(): pl.pallas_call(functools.partial(kernel, n_track, n_tile, tiles_here, pin...]
where the time goes in v5:
time: 49.5 us; the launch traced here: 49.3 us
  Pallas kernels  46.1 us (93%)
  local copies, waits for them, and re-layouts  2.55 us (5%)
  between operations  0.64 us (1%)
    pallas_call x1, Pallas kernels, on_device(): pl.pallas_call(functools.partial(kernel, n_track, n_tile, tiles_here, pin...  46.1 us
    unnamed x2, local copies, waits for them, and re-layouts  2.55 us

profile of v5, /device:TPU:1, one launch (start us, length us, event | category | flops | bytes accessed | tf_op | source)
XLA Modules:
  0.0 49.3 jit_solution(12906467746038434201)
XLA Ops:
  0.6 46.1 %shard_map.86 = (f32[4,2,1024]{2,1,0:T(2,128)}, f32[1,64]{1,0:T(1,128)}) custom-call(s32[4]{0:T(128)} %classes_hbm.1, s32[4]{0:T(128)} %counts_hbm.1, bf16[1024,1024]{1,0:T(8,128)(2,1)} %panels_hbm.1, f32[1,64]{1,0:T(1,128)} %bitcast.4, bf16[4,1024,512]{2,1,0:T(8,128)(2,1)} %weights_hbm.1, s32[6,128]{1,0:T(8,128)} %bitcast.3, s32[4,512]{1,0:T(4,128)} %foot_hbm.1), custom_call_target="tpu_custom_call" | custom-call | tf_op jit(solution)/shard_map/pallas_call | solution.py:407
  46.7 1.4 %copy.11 = f32[4,2,1024]{2,1,0:T(2,128)} copy(f32[4,2,1024]{2,1,0:T(2,128)} %get-tuple-element.8) | data formatting | bytes 65536
  48.1 1.2 %copy.12 = f32[64]{0:T(128)} copy(f32[64]{0:T(128)} %bitcast.5) | data formatting | bytes 512
